TPU v7x, 256 devices: a whole 4x4x8 slice. The times are simulated.
256 devices in a mesh: group: 32 (over x, y, core), dev: 8 (over z).
Axes of the slice: x: 4, y: 4, z: 8, core: 2. Of those that a mesh axis runs over, the one named last changes fastest.
Arguments:
- embeddings: bfloat16 [524288, 1024], P(('group', 'dev')), may hold values from -0.28125 to 0.28125
- nearest: float32 [524288], P(('group', 'dev')), may hold values from 0.5 to 32
- chosen: int32 [2, 512], replicated, may hold values from 0 to 524287, as said below
Outputs:
- nearest_after: float32 [524288], P(('group', 'dev'))
- round_costs: float32 [2], replicated
Inputs may be any that keep to these rules, and one draw needn't show every extreme that they name: `chosen`: in each round every device's rows (an aligned block of 2048 rows) hold at most 6 of the picks, and some device holds exactly 6; a row may be picked twice.
All inputs are finite; a program needn't handle non-finite values.
Results may differ from a plain program's by a relative error of at most 0.0003.
Values may be sent and summed in bfloat16 or wider, within the bound.
A program may use at most 64 MiB of HBM per device.

v0:
```python
import jax
import jax.numpy as jnp
from jax import lax
from jax.sharding import PartitionSpec as P


def absorb_rows(embeddings, row_norms, carry, cand_rows, cand_mask):
    cand_norm = jnp.sum(jnp.square(cand_rows.astype(jnp.float32)), axis=1)
    products = lax.dot_general(
        embeddings, cand_rows, (((1,), (1,)), ((), ())), preferred_element_type=jnp.float32
    )
    distance = jnp.maximum(row_norms[:, None] + cand_norm[None, :] - 2.0 * products, 0.0)
    distance = jnp.where(cand_mask[None, :] > 0, distance, jnp.inf)
    return jnp.minimum(carry, jnp.min(distance, axis=1))


def locate_picks(picked, shard_rows, position):
    owning = picked // shard_rows
    within = picked - owning * shard_rows
    return (within, owning == position)


def slot_table(embeddings, within, is_owned, capacity):
    ranking = jnp.cumsum(is_owned.astype(jnp.int32)) - 1
    table = (ranking[None, :] == jnp.arange(capacity, dtype=jnp.int32)[:, None]) & is_owned[None, :]
    slot_index = jnp.sum(jnp.where(table, within[None, :], 0), axis=1)
    filled = jnp.any(table, axis=1).astype(jnp.bfloat16)
    return (embeddings[slot_index], filled)


def local(embeddings, nearest, chosen):
    shard_rows = embeddings.shape[0]
    rounds = chosen.shape[0]
    cands = chosen.shape[1]
    groups = lax.axis_size("group")
    members = lax.axis_size("dev")
    devices = groups * members
    capacity = 3 * cands // (2 * devices) + 3
    position = lax.axis_index("group") * members + lax.axis_index("dev")
    all_rows = shard_rows * devices
    row_norms = jnp.sum(jnp.square(embeddings.astype(jnp.float32)), axis=1)
    batches = [[turn] for turn in range(rounds)]
    costs = []
    for batch in batches:
        located = [locate_picks(chosen[turn], shard_rows, position) for turn in batch]
        tables = [
            slot_table(embeddings, within, is_owned, capacity) for within, is_owned in located
        ]
        slot_rows = jnp.stack([entry[0] for entry in tables])
        filled = jnp.stack([entry[1] for entry in tables])
        start_carry = nearest[None, :]
        minima = jnp.stack(
            [
                absorb_rows(
                    embeddings,
                    row_norms,
                    start_carry[0],
                    lax.all_gather(slot_rows, ("group", "dev"), axis=1, tiled=True)[0],
                    lax.all_gather(filled, ("group", "dev"), axis=1, tiled=True)[0],
                )
            ]
        )
        fresh = minima[0]
        nearest = jnp.minimum(nearest, fresh)
        local_sum = jnp.sum(nearest)
        costs.append(lax.psum(local_sum, ("group", "dev")) / all_rows)
    round_costs = jnp.stack(costs)
    return (nearest, round_costs)


def solution(mesh):
    return jax.shard_map(
        local,
        mesh=mesh,
        in_specs=(P(("group", "dev"), None), P(("group", "dev")), P()),
        out_specs=(P(("group", "dev")), P()),
        check_vma=False,
    )
```

profile of v0, /device:TPU:1, one launch (start us, length us, event | category | flops | bytes accessed | tf_op | source)
XLA Modules:
  0.0 361.9 jit_solution(2718238228657545664)
XLA Ops:
  7.2 0.0 all-gather.9.cloned.1.call-start
  7.2 0.7 compare_reduce_fusion
  7.9 0.8 multiply_subtract_fusion.1
  8.8 0.3 reduce-window.16
  9.1 0.1 slice.21
  9.2 0.1 slice_reduce_fusion.1
  9.3 0.1 add_bitcast_fusion.1
  9.4 0.1 select_reduce_fusion.1
  9.5 3.9 %gather_fusion = bf16[6,1024]{1,0:T(8,128)(2,1)} fusion(bf16[2048,1024]{1,0:T(8,128)(2,1)} %param.3, s32[1024]{0:T(1024)S(1)} %pad_clamp_fusion.1), kind=kCustom, calls=%fused_computation | custom fusion | bytes 24600 | tf_op jit(solution)/shard_map/gather | solution.py:28
  13.4 0.0 all-gather.9.cloned.1.call-update
  13.4 0.0 all-gather.11.cloned.1.call-start
  13.5 0.3 reduce-window.24
  13.8 0.1 slice.24
  13.9 0.1 slice_reduce_fusion
  14.0 0.1 add_bitcast_fusion
  14.1 0.1 select_reduce_fusion
  14.2 3.9 %gather_fusion.1 = bf16[6,1024]{1,0:T(8,128)(2,1)} fusion(bf16[2048,1024]{1,0:T(8,128)(2,1)} %param.3, s32[1024]{0:T(1024)S(1)} %pad_clamp_fusion), kind=kCustom, calls=%fused_computation.1 | custom fusion | bytes 24600 | tf_op jit(solution)/shard_map/gather | solution.py:28
  18.1 0.0 all-gather.11.cloned.1.call-update
  18.2 0.1 fusion.7
  18.3 0.1 fusion.9
  18.5 0.2 dynamic-update-slice
  18.7 0.2 dynamic-update-slice.1
  18.9 82.1 %all-reduce.3 = (bf16[1536]{0:T(1024)(128)(2,1)S(1)}, bf16[1536]{0:T(1024)(128)(2,1)S(1)}) all-reduce(bf16[1536]{0:T(1024)(128)(2,1)S(1)} %dynamic-update-slice.1, bf16[1536]{0:T(1024)(128)(2,1)S(1)} %dynamic-update-slice), channel_id=4, replica_groups=mesh['group'=32,'dev'=8] {'group','dev'}, use_global_device_ids=true, to_apply=%add.1 | all-reduce | flops 3072 | bytes 12288
  101.1 3.3 multiply_reduce_fusion
  104.4 28.6 %all-gather.9.cloned.1.call-done = bf16[256,6,1024]{2,1,0:T(8,128)(2,1)} async-done(((bf16[1,6,1024]{2,1,0:T(8,128)(2,1)}), bf16[256,6,1024]{2,1,0:T(8,128)(2,1)}) %all-gather.9.cloned.1.call-update) | async-done | bytes 3145744 | tf_op jit(solution)/shard_map/all_gather | solution.py:58
  133.0 4.9 %reshape.154 = bf16[1536,1024]{1,0:T(8,128)(2,1)S(1)} reshape(bf16[256,6,1024]{2,1,0:T(8,128)(2,1)} %all-gather.9.cloned.1.call-done) | data formatting | bytes 6291456
  137.9 0.7 multiply_reduce_fusion.2
  138.6 110.6 %all-gather.11.cloned.1.call-done = bf16[256,6,1024]{2,1,0:T(8,128)(2,1)} async-done(((bf16[1,6,1024]{2,1,0:T(8,128)(2,1)}), bf16[256,6,1024]{2,1,0:T(8,128)(2,1)}) %all-gather.11.cloned.1.call-update) | async-done | bytes 3145744 | tf_op jit(solution)/shard_map/all_gather | solution.py:58
  249.2 6.3 %reshape.156 = bf16[1536,1024]{1,0:T(8,128)(2,1)} reshape(bf16[256,6,1024]{2,1,0:T(8,128)(2,1)} %all-gather.11.cloned.1.call-done) | data formatting | bytes 6291456
  255.5 2.6 multiply_reduce_fusion.1
  258.1 0.0 copy-start
  258.1 0.0 copy-start.1
  258.1 10.6 %fusion.5 = f32[2048]{0:T(1024)S(1)} fusion(bf16[1536,1024]{1,0:T(8,128)(2,1)S(1)} %reshape.154, bf16[2048,1024]{1,0:T(8,128)(2,1)} %param.3, f32[1536]{0:T(1024)S(1)} %multiply_reduce_fusion.2, f32[2048]{0:T(1024)S(1)} %multiply_reduce_fusion, pred[1536]{0:T(1024)(128)(4,1)S(1)} %broadcast_compare_fusion.1), kind=kOutput, calls=%fused_computation.9 | convolution fusion | flops 6461323264 | bytes 7364096 | tf_op jit(solution)/shard_map/dot_general | solution.py:9
  268.7 0.0 copy-done
  268.7 0.0 copy-done.1
  268.7 0.0 copy-start.2
  268.7 8.4 %fusion.2 = f32[2048]{0:T(1024)S(1)} fusion(bf16[1536,1024]{1,0:T(8,128)(2,1)S(1)} %copy-done, bf16[2048,1024]{1,0:T(8,128)(2,1)S(1)} %copy-done.1, f32[1536]{0:T(1024)S(1)} %multiply_reduce_fusion.1, f32[2048]{0:T(1024)S(1)} %multiply_reduce_fusion, pred[1536]{0:T(1024)(128)(4,1)S(1)} %broadcast_compare_fusion), kind=kOutput, calls=%fused_computation.5 | convolution fusion | flops 6461323264 | bytes 7364096 | tf_op jit(solution)/shard_map/dot_general | solution.py:9
  277.1 0.0 copy-done.2
  277.1 1.2 fusion.20
  278.3 74.8 %all-reduce.2 = (f32[]{:T(128)}, f32[]{:T(128)}) all-reduce(f32[]{:T(128)} %get-tuple-element.6, f32[]{:T(128)} %get-tuple-element.12), channel_id=1, replica_groups=mesh['group'=32,'dev'=8] {'group','dev'}, use_global_device_ids=true, to_apply=%region_16.17 | all-reduce | flops 2 | bytes 16 | tf_op jit(solution)/shard_map/psum | solution.py:66
  354.5 0.6 pad_maximum_fusion
  (14 shorter events, 0.2 us)
Async XLA Ops:
  7.2 125.8 %all-gather.9.cloned.1.call-start = ((), (), s32[]{:S(2)}) async-start(), calls=%async_computation | async-start | bytes 4210688 | tf_op jit(solution)/shard_map/all_gather | solution.py:58
  13.4 235.7 %all-gather.11.cloned.1.call-start = ((), (), s32[]{:S(2)}) async-start(), calls=%async_computation.1 | async-start | bytes 4210688 | tf_op jit(solution)/shard_map/all_gather | solution.py:58
  258.1 10.6 %copy-start = (bf16[1536,1024]{1,0:T(8,128)(2,1)S(1)}, bf16[1536,1024]{1,0:T(8,128)(2,1)}, u32[]{:S(2)}) copy-start(bf16[1536,1024]{1,0:T(8,128)(2,1)} %reshape.156) | copy-start | bytes 9437188
  258.1 10.6 %copy-start.1 = (bf16[2048,1024]{1,0:T(8,128)(2,1)S(1)}, bf16[2048,1024]{1,0:T(8,128)(2,1)}, u32[]{:S(2)}) copy-start(bf16[2048,1024]{1,0:T(8,128)(2,1)} %param.3) | copy-start | bytes 12582916
  268.7 8.4 %copy-start.2 = (f32[2048]{0:T(1024)S(1)}, f32[2048]{0:T(1024)}, u32[]{:S(2)}) copy-start(f32[2048]{0:T(1024)} %param.4) | copy-start | bytes 24580
Sparse Core Ops, SparseCore 0:
  13.6 119.4 all-gather.8
  136.7 112.4 all-gather.10
where the time goes:
time: 363 us; the launch traced here: 362 us
  blocking collectives  157 us (43%)
  waiting for transfers between devices  139 us (38%)
  local copies, waits for them, and re-layouts  19.9 us (5%)
  matrix products  18.9 us (5%)
  between operations  15.5 us (4%)
  other arithmetic  11.3 us (3%)
    all_gather x2, waiting for transfers between devices, local(): lax.all_gather(slot_rows, ('group', 'dev'), axis=1, tiled=True)[0]  139 us
    unnamed x1, blocking collectives  82.1 us
    psum x1, blocking collectives, local(): costs.append(lax.psum(local_sum, ('group', 'dev')) / all_rows)  74.8 us
    dot_general x2, matrix products, absorb_rows(): lax.dot_general(embeddings, cand_rows, (((1,), (1,)), ((), ())), preferre...  18.9 us
    unnamed x12, local copies, waits for them, and re-layouts  11.7 us
    gather x2, local copies, waits for them, and re-layouts, slot_table(): return (embeddings[slot_index], filled)  7.8 us
  transfers between devices with their start and end apart: 2, of which 2 were waited for; matrix products, arithmetic and copies ran while one was open for 4% of the time, Pallas kernels for 0%

commit v1 on v0

v1 whole, which is shorter than its diff:
```python
import functools

import jax
import jax.numpy as jnp
from jax import lax
from jax.experimental import pallas as pl
from jax.experimental.pallas import tpu as pltpu
from jax.sharding import PartitionSpec as P

MESH = pl.DeviceIdType.MESH
NT = (((1,), (1,)), ((), ()))
NX, NY = 4, 4
MOST = 6
FAR = 2.0**50
NONE = 2**30
TILE = 256


def place():
    group = lax.axis_index("group")
    return group // (2 * NY), (group // 2) % NY, group % 2, lax.axis_index("dev")


def device(x, y, c, z):
    return ((x * NY + y) * 2 + c, z)


def picked_rows(chosen_ref, emb_ref, position):
    rows = emb_ref.shape[0] * 16
    cands = chosen_ref.shape[1]
    chosen = chosen_ref[...]
    order = lax.broadcasted_iota(jnp.int32, chosen.shape, 1)
    within = chosen - position * rows
    owned = (within >= 0) & (within < rows)
    key = jnp.where(owned, within * cands + order, NONE)
    found = [[], []]
    line = lax.broadcasted_iota(jnp.int32, (16, emb_ref.shape[2]), 0)
    for _ in range(MOST):
        least = jnp.min(key, axis=1, keepdims=True)
        key = jnp.where(key == least, NONE, key)
        tile = jnp.minimum(least, rows * cands - 1) // (16 * cands)
        inside = least // cands - tile * 16
        for turn in range(2):
            block = emb_ref[tile[turn, 0]].astype(jnp.float32)
            chosen_line = line == inside[turn : turn + 1, :]
            row = jnp.sum(jnp.where(chosen_line, block, 0.0), axis=0, keepdims=True)
            found[turn].append(jnp.where(least[turn : turn + 1, :] < NONE, row * -2.0, FAR))
    return found


def kernel(
    chosen_ref, near_ref, emb_hbm, out_ref, cost_ref,
    emb, col, cand, least, sum_z, sum_xy,
    emb_sem, zs, zr, bs, cs, ks, slab_r, sib_r, azs, azr, axs, axr, total_rows,
):
    x, y, c, z = place()
    nz = lax.axis_size("dev")
    position = lax.axis_index("group") * nz + z
    rows = emb.shape[0] * 16
    slab = nz * MOST
    major, minor = (y, x), (x, y)

    load = pltpu.make_async_copy(emb_hbm, emb, emb_sem)
    load.start()

    column = [((z + dz) % nz, (c + dc) % 2) for dz in range(nz) for dc in range(2) if dz or dc]
    plane = [((x + dx) % NX, (y + dy) % NY) for dx in range(NX) for dy in range(NY) if dx or dy]
    barrier = pltpu.get_barrier_semaphore()
    for tz, tc in column:
        pl.semaphore_signal(barrier, inc=1, device_id=device(x, y, tc, tz), device_id_type=MESH)
    for tx, ty in plane:
        pl.semaphore_signal(barrier, inc=1, device_id=device(tx, ty, c, z), device_id_type=MESH)

    least[...] = jnp.full(least.shape, jnp.inf, jnp.float32)
    load.wait()
    found = picked_rows(chosen_ref, emb, position)
    pad = jnp.zeros((4, emb.shape[2]), jnp.float32)
    col[z] = jnp.concatenate(found[0] + found[1] + [pad], axis=0).astype(jnp.bfloat16)
    pl.semaphore_wait(barrier, len(column) + len(plane))

    def z_copy(k):
        return pltpu.make_async_remote_copy(
            src_ref=col.at[z], dst_ref=col.at[z], send_sem=zs.at[k - 1], recv_sem=zr.at[z],
            device_id=device(x, y, c, (z + k) % nz), device_id_type=MESH)

    def z_arrival(k):
        t = (z + k) % nz
        return pltpu.make_async_remote_copy(
            src_ref=col.at[t], dst_ref=col.at[t], send_sem=zs.at[k - 1], recv_sem=zr.at[t],
            device_id=device(x, y, c, t), device_id_type=MESH)

    for k in (4, 3, 5, 2, 6, 1, 7):
        z_copy(k).start()

    for j in range(rows // 128):
        part = emb[8 * j : 8 * (j + 1)].reshape(128, -1).astype(jnp.float32)
        part = part * part
        part = sum(part[:, 128 * i : 128 * (i + 1)] for i in range(part.shape[1] // 128))
        out_ref[:, 128 * j : 128 * (j + 1)] = jnp.sum(part.T, axis=0, keepdims=True)

    for k in range(1, nz):
        z_arrival(k).wait_recv()

    whole = [col[t].astype(jnp.float32) for t in range(nz)]
    for p in range(2):
        packed = jnp.concatenate([w[MOST * p : MOST * (p + 1), :] for w in whole], axis=0)
        start = pl.multiple_of((minor[p] * 2 + c) * slab, 16)
        cand[p, major[p], pl.ds(start, slab), :] = packed.astype(jnp.bfloat16)

    def slab_at(p, a, b, core):
        start = pl.multiple_of((b * 2 + core) * slab, 16)
        return cand.at[p, a, pl.ds(start, slab), :]

    def spot(p, a, b):
        return (b, a) if p == 0 else (a, b)

    def copy(p, a, b, core, ssem, rsem, target):
        ref = slab_at(p, a, b, core)
        return pltpu.make_async_remote_copy(
            src_ref=ref, dst_ref=ref, send_sem=ssem, recv_sem=rsem,
            device_id=target, device_id_type=MESH)

    def major_copy(p, k):
        a, b = major[p], minor[p]
        tx, ty = spot(p, (a + k) % 4, b)
        return copy(p, a, b, c, bs.at[p, k - 1], slab_r.at[p, a, b], device(tx, ty, c, z))

    def minor_copy(p, a, k):
        b = minor[p]
        tx, ty = spot(p, major[p], (b + k) % 4)
        return copy(p, a, b, c, cs.at[p, a, k - 1], slab_r.at[p, a, b], device(tx, ty, c, z))

    def core_copy(p, a, b):
        return copy(p, a, b, c, ks.at[p, a, b], sib_r.at[p, a, b], device(x, y, 1 - c, z))

    def slab_arrival(p, a, b):
        return copy(p, a, b, c, ks.at[p, a, b], slab_r.at[p, a, b], device(x, y, 1 - c, z))

    def core_arrival(p, a, b):
        return copy(p, a, b, 1 - c, ks.at[p, a, b], sib_r.at[p, a, b], device(x, y, 1 - c, z))

    for k in (2, 1, 3):
        for p in range(2):
            major_copy(p, k).start()
    for p in range(2):
        for k in (2, 1, 3):
            minor_copy(p, major[p], k).start()
        core_copy(p, major[p], minor[p]).start()
    for k in (1, 3, 2):
        for p in range(2):
            a = (major[p] + k) % 4
            slab_arrival(p, a, minor[p]).wait_recv()
            for j in (2, 1, 3):
                minor_copy(p, a, j).start()
            core_copy(p, a, minor[p]).start()

    def turn_at(p, k):
        return (major[p] + k + (k // 2) * (1 - 2 * (k % 2))) % 4

    def pass_on(p, k):
        a = turn_at(p, k)
        for j in (1, 3, 2):
            b = (minor[p] + j) % 4
            slab_arrival(p, a, b).wait_recv()
            core_copy(p, a, b).start()

    def absorb(p, k):
        a = turn_at(p, k)
        for b in range(4):
            core_arrival(p, a, b).wait_recv()
        block = cand[p, a]
        wide = block.astype(jnp.float32)
        norm = jnp.sum(wide * wide, axis=1, keepdims=True) * 0.25
        for j in range(rows // TILE):
            lanes = slice(TILE * j, TILE * (j + 1))
            mine = emb[TILE // 16 * j : TILE // 16 * (j + 1)].reshape(TILE, -1)
            product = lax.dot_general(block, mine, NT, preferred_element_type=jnp.float32)
            reach = (product + norm).reshape(-1, 8, TILE)
            least[p, :, lanes] = jnp.minimum(least[p, :, lanes], jnp.min(reach, axis=0))

    for p in range(2):
        pass_on(p, 0)

    def step(k, _):
        for p in range(2):
            absorb(p, k)

            @pl.when(k < 3)
            def _():
                pass_on(p, k + 1)

        return 0

    lax.fori_loop(0, 4, step, 0)

    norms = out_ref[...]
    near = near_ref[...]
    sums = []
    for p in range(2):
        reach = jnp.min(least[p], axis=0, keepdims=True)
        near = jnp.minimum(near, jnp.maximum(norms + reach, 0.0))
        sums.append(jnp.sum(near, axis=1, keepdims=True))
    lane = lax.broadcasted_iota(jnp.int32, (1, 128), 1)
    share = jnp.where(lane == 0, sums[0], jnp.where(lane == 1, sums[1], 0.0))

    at_z = z * 2 + c
    sum_z[at_z] = share
    for i, (tz, tc) in enumerate(column):
        pltpu.make_async_remote_copy(
            src_ref=sum_z.at[at_z], dst_ref=sum_z.at[at_z], send_sem=azs.at[i],
            recv_sem=azr.at[at_z], device_id=device(x, y, tc, tz), device_id_type=MESH).start()
    out_ref[...] = near
    for i, (tz, tc) in enumerate(column):
        t = tz * 2 + tc
        pltpu.make_async_remote_copy(
            src_ref=sum_z.at[t], dst_ref=sum_z.at[t], send_sem=azs.at[i],
            recv_sem=azr.at[t], device_id=device(x, y, tc, tz), device_id_type=MESH).wait_recv()
    at_xy = x * NY + y
    sum_xy[at_xy] = jnp.sum(sum_z[...], axis=0)
    for i, (tx, ty) in enumerate(plane):
        pltpu.make_async_remote_copy(
            src_ref=sum_xy.at[at_xy], dst_ref=sum_xy.at[at_xy], send_sem=axs.at[i],
            recv_sem=axr.at[at_xy], device_id=device(tx, ty, c, z), device_id_type=MESH).start()

    for k in range(1, nz):
        z_copy(k).wait_send()
    for p in range(2):
        for k in (1, 2, 3):
            major_copy(p, k).wait_send()
        for a in range(4):
            for k in (1, 2, 3):
                minor_copy(p, a, k).wait_send()
            for b in range(4):
                core_copy(p, a, b).wait_send()
    for i, (tz, tc) in enumerate(column):
        pltpu.make_async_remote_copy(
            src_ref=sum_z.at[at_z], dst_ref=sum_z.at[at_z], send_sem=azs.at[i],
            recv_sem=azr.at[at_z], device_id=device(x, y, tc, tz), device_id_type=MESH).wait_send()

    for i, (tx, ty) in enumerate(plane):
        t = tx * NY + ty
        both = pltpu.make_async_remote_copy(
            src_ref=sum_xy.at[t], dst_ref=sum_xy.at[t], send_sem=axs.at[i],
            recv_sem=axr.at[t], device_id=device(tx, ty, c, z), device_id_type=MESH)
        both.wait_recv()
        both.wait_send()
    final = jnp.sum(sum_xy[...], axis=0) / total_rows
    cost_ref[0] = final[0, 0]
    cost_ref[1] = final[0, 1]


def local(embeddings, nearest, chosen):
    rows, width = embeddings.shape
    nz = lax.axis_size("dev")
    total_rows = rows * nz * lax.axis_size("group")
    dma = pltpu.SemaphoreType.DMA

    near, cost = pl.pallas_call(
        functools.partial(kernel, total_rows=total_rows),
        out_shape=(
            jax.ShapeDtypeStruct((1, rows), jnp.float32),
            jax.ShapeDtypeStruct((2,), jnp.float32),
        ),
        in_specs=[
            pl.BlockSpec(memory_space=pltpu.VMEM),
            pl.BlockSpec(memory_space=pltpu.VMEM),
            pl.BlockSpec(memory_space=pl.ANY),
        ],
        out_specs=(
            pl.BlockSpec(memory_space=pltpu.VMEM),
            pl.BlockSpec(memory_space=pltpu.SMEM),
        ),
        scratch_shapes=[
            pltpu.VMEM((rows // 16, 16, width), jnp.bfloat16),
            pltpu.VMEM((nz, 16, width), jnp.bfloat16),
            pltpu.VMEM((2, 4, 8 * nz * MOST, width), jnp.bfloat16),
            pltpu.VMEM((2, 8, rows), jnp.float32),
            pltpu.VMEM((2 * nz, 1, 128), jnp.float32),
            pltpu.VMEM((NX * NY, 1, 128), jnp.float32),
            dma,
            dma((nz - 1,)),
            dma((nz,)),
            dma((2, 3)),
            dma((2, 4, 3)),
            dma((2, 4, 4)),
            dma((2, 4, 4)),
            dma((2, 4, 4)),
            dma((2 * nz - 1,)),
            dma((2 * nz,)),
            dma((NX * NY - 1,)),
            dma((NX * NY,)),
        ],
        compiler_params=pltpu.CompilerParams(
            collective_id=0, has_side_effects=True, vmem_limit_bytes=40 * 2**20
        ),
        cost_estimate=pl.CostEstimate(
            flops=2 * rows * width * 3072, bytes_accessed=rows * width * 2, transcendentals=0
        ),
    )(chosen, nearest.reshape(1, rows), embeddings.reshape(rows // 16, 16, width))
    return near.reshape(rows), cost


def solution(mesh):
    return jax.shard_map(
        local,
        mesh=mesh,
        in_specs=(P(("group", "dev"), None), P(("group", "dev")), P()),
        out_specs=(P(("group", "dev")), P()),
        check_vma=False,
    )
```

time: 363 us -> 64.8 us (0.18)
  blocking collectives: 157 us -> 0 us
  waiting for transfers between devices: 139 us -> 0 us
  Pallas kernels: 0 us -> 59.3 us
  matrix products: 18.9 us -> 0 us
  local copies, waits for them, and re-layouts: 19.9 us -> 4.68 us
  between operations: 15.5 us -> 0.65 us
  other arithmetic: 11.3 us -> 0 us
    all_gather x2 -> x0, waiting for transfers between devices: 139 us -> none  [local(): lax.all_gather(slot_rows, ('group', 'dev'), axis=1, tiled=True)[0]]
    unnamed x1 -> x0, blocking collectives: 82.1 us -> none
    psum x1 -> x0, blocking collectives: 74.8 us -> none  [local(): costs.append(lax.psum(local_sum, ('group', 'dev')) / all_rows)]
    pallas_call x0 -> x1, Pallas kernels: none -> 59.3 us  [local(): pl.pallas_call(functools.partial(kernel, total_rows=total_rows), out_shap...]
    dot_general x2 -> x0, matrix products: 18.9 us -> none  [absorb_rows(): lax.dot_general(embeddings, cand_rows, (((1,), (1,)), ((), ())), preferre...]
    reduce_sum x6 -> x0, other arithmetic: 8.01 us -> none  [the longest x1 3.31 us: local(): row_norms = jnp.sum(jnp.square(embeddings.astype(jnp.float32)), axis=1)]
    gather x2 -> x0, local copies, waits for them, and re-layouts: 7.8 us -> none  [slot_table(): return (embeddings[slot_index], filled)]
    unnamed x12 -> x8, local copies, waits for them, and re-layouts: 11.7 us -> 4.68 us
  transfers between devices with their start and end apart: 2 -> 0, of which waited for: 2 -> 0; matrix products, arithmetic and copies ran while one was open for 4% -> 0% of each run, Pallas kernels for 0% -> 0%
where the time goes in v1:
time: 64.8 us; the launch traced here: 64.6 us
  Pallas kernels  59.3 us (92%)
  local copies, waits for them, and re-layouts  4.68 us (7%)
  between operations  0.65 us (1%)
    pallas_call x1, Pallas kernels, local(): pl.pallas_call(functools.partial(kernel, total_rows=total_rows), out_shap...  59.3 us
    unnamed x8, local copies, waits for them, and re-layouts  4.68 us

profile of v1, /device:TPU:1, one launch (start us, length us, event | category | flops | bytes accessed | tf_op | source)
XLA Modules:
  0.0 64.6 jit_solution(1093013639514957473)
XLA Ops:
  0.6 0.0 copy-start
  0.6 2.2 %copy-done = bf16[2048,1024]{1,0:T(8,128)(2,1)S(1)} copy-done((bf16[2048,1024]{1,0:T(8,128)(2,1)S(1)}, bf16[2048,1024]{1,0:T(8,128)(2,1)}, u32[]{:S(2)}) %copy-start) | copy-done | bytes 4194328
  2.8 0.0 copy-start.1
  2.8 0.7 %copy-done.1 = f32[2048]{0:T(1024)S(1)} copy-done((f32[2048]{0:T(1024)S(1)}, f32[2048]{0:T(1024)}, u32[]{:S(2)}) %copy-start.1) | copy-done | bytes 8216
  3.5 0.0 copy-start.2
  3.5 0.7 %copy-done.2 = s32[2,512]{1,0:T(2,128)S(1)} copy-done((s32[2,512]{1,0:T(2,128)S(1)}, s32[2,512]{1,0:T(2,128)}, u32[]{:S(2)}) %copy-start.2) | copy-done | bytes 4120
  4.2 59.3 %shard_map.50 = (f32[1,2048]{1,0:T(1,128)S(1)}, f32[2]{0:T(128)S(1)}) custom-call(s32[2,512]{1,0:T(2,128)S(1)} %copy-done.2, f32[1,2048]{1,0:T(1,128)S(1)} %bitcast.5, bf16[128,16,1024]{2,1,0:T(8,128)(2,1)S(1)} %bitcast.4), custom_call_target="tpu_custom_call" | custom-call | flops 12884901888 | bytes 4194304 | tf_op jit(solution)/shard_map/pallas_call | solution.py:258
  63.5 0.6 copy.7
  64.1 0.5 copy.8
Async XLA Ops:
  0.6 2.2 %copy-start = (bf16[2048,1024]{1,0:T(8,128)(2,1)S(1)}, bf16[2048,1024]{1,0:T(8,128)(2,1)}, u32[]{:S(2)}) copy-start(bf16[2048,1024]{1,0:T(8,128)(2,1)} %param.3) | copy-start | bytes 12582916
  2.8 0.7 %copy-start.1 = (f32[2048]{0:T(1024)S(1)}, f32[2048]{0:T(1024)}, u32[]{:S(2)}) copy-start(f32[2048]{0:T(1024)} %param.4) | copy-start | bytes 24580
  3.5 0.7 %copy-start.2 = (s32[2,512]{1,0:T(2,128)S(1)}, s32[2,512]{1,0:T(2,128)}, u32[]{:S(2)}) copy-start(s32[2,512]{1,0:T(2,128)} %chosen_ref.1) | copy-start | bytes 12292

commit v2 on v1

--- a/solution.py
+++ b/solution.py
@@ -11,7 +11,6 @@
 NT = (((1,), (1,)), ((), ()))
 NX, NY = 4, 4
 MOST = 6
-FAR = 2.0**50
 NONE = 2**30
 TILE = 256
 
@@ -25,43 +24,77 @@
     return ((x * NY + y) * 2 + c, z)
 
 
-def picked_rows(chosen_ref, emb_ref, position):
-    rows = emb_ref.shape[0] * 16
-    cands = chosen_ref.shape[1]
-    chosen = chosen_ref[...]
+def find_picks(chosen, position, rows):
+    cands = chosen.shape[1]
     order = lax.broadcasted_iota(jnp.int32, chosen.shape, 1)
     within = chosen - position * rows
     owned = (within >= 0) & (within < rows)
     key = jnp.where(owned, within * cands + order, NONE)
-    found = [[], []]
-    line = lax.broadcasted_iota(jnp.int32, (16, emb_ref.shape[2]), 0)
+    found = []
     for _ in range(MOST):
         least = jnp.min(key, axis=1, keepdims=True)
         key = jnp.where(key == least, NONE, key)
-        tile = jnp.minimum(least, rows * cands - 1) // (16 * cands)
-        inside = least // cands - tile * 16
-        for turn in range(2):
+        index = jnp.minimum(least, rows * cands - 1) // cands
+        tile = index // 16
+        found.append((tile, index - tile * 16))
+    return found
+
+
+def picked_rows(found, emb_ref):
+    line = lax.broadcasted_iota(jnp.int32, (16, emb_ref.shape[2]), 0)
+    picked = []
+    for turn in range(2):
+        for tile, inside in found:
             block = emb_ref[tile[turn, 0]].astype(jnp.float32)
-            chosen_line = line == inside[turn : turn + 1, :]
-            row = jnp.sum(jnp.where(chosen_line, block, 0.0), axis=0, keepdims=True)
-            found[turn].append(jnp.where(least[turn : turn + 1, :] < NONE, row * -2.0, FAR))
-    return found
+            here = line == inside[turn : turn + 1, :]
+            picked.append(jnp.sum(jnp.where(here, block, 0.0), axis=0, keepdims=True) * -2.0)
+    return jnp.concatenate(picked, axis=0)
+
+
+def slot_sources(chosen_ref, x, y, z, rows, nz):
+    cands = chosen_ref.shape[1]
+    per = 2 * cands // nz
+    turn = z // (nz // 2)
+    start = (z % (nz // 2)) * per
+    every = chosen_ref[0:1, :] * (1 - turn) + chosen_ref[1:2, :] * turn
+    order = lax.broadcasted_iota(jnp.int32, (per, cands), 1)
+    place_in = lax.broadcasted_iota(jnp.int32, (per, cands), 0) + start
+    mine = jnp.sum(jnp.where(order == place_in, every, 0), axis=1, keepdims=True)
+    owner = mine // rows
+    earlier = (every < mine) | ((every == mine) & (order < place_in))
+    rank = jnp.sum(jnp.where((every // rows == owner) & earlier, 1, 0), axis=1, keepdims=True)
+    slot = turn * MOST + rank
+    group = owner // nz
+    source = ((owner - group * nz) * 2 + group % 2) * 16
+    here = group // 2 == x * NY + y
+    lane = lax.broadcasted_iota(jnp.int32, (per, 32 * nz), 1)
+    main = (here & (lane == source + slot)).astype(jnp.bfloat16)
+    low = here & (lane == source + 12 + slot % 4)
+    tails = [(low & (slot // 4 == i)).astype(jnp.bfloat16) for i in range(3)]
+    return main, tails
 
 
 def kernel(
-    chosen_ref, near_ref, emb_hbm, out_ref, cost_ref,
-    emb, col, cand, least, sum_z, sum_xy,
-    emb_sem, zs, zr, bs, cs, ks, slab_r, sib_r, azs, azr, axs, axr, total_rows,
+    chosen_hbm, near_hbm, emb_hbm, out_ref, cost_ref,
+    chosen_ref, near_ref, emb, sent, col, parts, shares, ours, cand, least, sum_z, sum_xy,
+    in_sem, zs, zr, ps, pr, os, orr, bs, cs, ks, slab_r, sib_r, azs, azr, axs, axr, total_rows,
 ):
     x, y, c, z = place()
     nz = lax.axis_size("dev")
     position = lax.axis_index("group") * nz + z
     rows = emb.shape[0] * 16
-    slab = nz * MOST
+    slab = 4 * nz
+    half = emb.shape[2] // 2
+    cut = 3 * half // 4
+    at_z, at_xy = z * 2 + c, x * NY + y
     major, minor = (y, x), (x, y)
 
-    load = pltpu.make_async_copy(emb_hbm, emb, emb_sem)
+    load = pltpu.make_async_copy(emb_hbm, emb, in_sem.at[0])
+    load_chosen = pltpu.make_async_copy(chosen_hbm, chosen_ref, in_sem.at[1])
+    load_near = pltpu.make_async_copy(near_hbm, near_ref, in_sem.at[2])
+    load_chosen.start()
     load.start()
+    load_near.start()
 
     column = [((z + dz) % nz, (c + dc) % 2) for dz in range(nz) for dc in range(2) if dz or dc]
     plane = [((x + dx) % NX, (y + dy) % NY) for dx in range(NX) for dy in range(NY) if dx or dy]
@@ -72,25 +105,34 @@
         pl.semaphore_signal(barrier, inc=1, device_id=device(tx, ty, c, z), device_id_type=MESH)
 
     least[...] = jnp.full(least.shape, jnp.inf, jnp.float32)
+    load_chosen.wait()
+    picks = find_picks(chosen_ref[...], position, rows)
     load.wait()
-    found = picked_rows(chosen_ref, emb, position)
-    pad = jnp.zeros((4, emb.shape[2]), jnp.float32)
-    col[z] = jnp.concatenate(found[0] + found[1] + [pad], axis=0).astype(jnp.bfloat16)
+    found = picked_rows(picks, emb)
+    for h in range(2):
+        wide = found[:, half * h : half * (h + 1)]
+        tail = jnp.concatenate([wide[4 * i : 4 * i + 4, cut:] for i in range(3)], axis=1)
+        sent[h] = jnp.concatenate([wide[:, :cut], tail], axis=0).astype(jnp.bfloat16)
+    col[at_z] = sent[c]
     pl.semaphore_wait(barrier, len(column) + len(plane))
 
-    def z_copy(k):
+    def remote(src, dst, ssem, rsem, target):
         return pltpu.make_async_remote_copy(
-            src_ref=col.at[z], dst_ref=col.at[z], send_sem=zs.at[k - 1], recv_sem=zr.at[z],
-            device_id=device(x, y, c, (z + k) % nz), device_id_type=MESH)
-
-    def z_arrival(k):
-        t = (z + k) % nz
-        return pltpu.make_async_remote_copy(
-            src_ref=col.at[t], dst_ref=col.at[t], send_sem=zs.at[k - 1], recv_sem=zr.at[t],
-            device_id=device(x, y, c, t), device_id_type=MESH)
-
-    for k in (4, 3, 5, 2, 6, 1, 7):
-        z_copy(k).start()
+            src_ref=src, dst_ref=dst, send_sem=ssem, recv_sem=rsem,
+            device_id=target, device_id_type=MESH)
+
+    def slots_copy(i):
+        tz, tc = column[i]
+        return remote(sent.at[tc], col.at[at_z], zs.at[i], zr.at[at_z], device(x, y, tc, tz))
+
+    def slots_arrival(i):
+        tz, tc = column[i]
+        t = tz * 2 + tc
+        return remote(sent.at[tc], col.at[t], zs.at[i], zr.at[t], device(x, y, tc, tz))
+
+    far_first = sorted(range(len(column)), key=lambda i: abs((i + 1) // 2 - nz // 2))
+    for i in far_first:
+        slots_copy(i).start()
 
     for j in range(rows // 128):
         part = emb[8 * j : 8 * (j + 1)].reshape(128, -1).astype(jnp.float32)
@@ -98,27 +140,68 @@
         part = sum(part[:, 128 * i : 128 * (i + 1)] for i in range(part.shape[1] // 128))
         out_ref[:, 128 * j : 128 * (j + 1)] = jnp.sum(part.T, axis=0, keepdims=True)
 
+    main, tails = slot_sources(chosen_ref, x, y, z, rows, nz)
+    for i in range(len(column)):
+        slots_arrival(i).wait_recv()
+
+    gathered = col[...].reshape(-1, cut)
+    left = jnp.dot(main, gathered, preferred_element_type=jnp.float32)
+    right = sum(
+        jnp.dot(tail, gathered[:, 128 * i : 128 * (i + 1)], preferred_element_type=jnp.float32)
+        for i, tail in enumerate(tails)
+    )
+    dense = jnp.concatenate([left, right], axis=1)
+    for t in range(NX * NY):
+        rows8 = dense[8 * t : 8 * t + 8]
+        both = jnp.concatenate([rows8[:, : half // 2], rows8[:, half // 2 :]], axis=0)
+        parts[t] = both.astype(jnp.bfloat16)
+    shares[at_xy] = parts[at_xy]
+
+    def part_copy(i):
+        tx, ty = plane[i]
+        t = tx * NY + ty
+        return remote(parts.at[t], shares.at[at_xy], ps.at[i], pr.at[at_xy], device(tx, ty, c, z))
+
+    def part_arrival(i):
+        tx, ty = plane[i]
+        t = tx * NY + ty
+        return remote(parts.at[t], shares.at[t], ps.at[i], pr.at[t], device(tx, ty, c, z))
+
+    for i in range(len(plane)):
+        part_copy(i).start()
+    for i in range(len(plane)):
+        part_arrival(i).wait_recv()
+    ours[z] = jnp.sum(shares[...].astype(jnp.float32), axis=0).astype(jnp.bfloat16)
+
+    def z_copy(k):
+        return remote(ours.at[z], ours.at[z], os.at[k - 1], orr.at[z], device(x, y, c, (z + k) % nz))
+
+    def z_arrival(k):
+        t = (z + k) % nz
+        return remote(ours.at[t], ours.at[t], os.at[k - 1], orr.at[t], device(x, y, c, t))
+
+    for k in (4, 3, 5, 2, 6, 1, 7):
+        z_copy(k).start()
     for k in range(1, nz):
         z_arrival(k).wait_recv()
-
-    whole = [col[t].astype(jnp.float32) for t in range(nz)]
     for p in range(2):
-        packed = jnp.concatenate([w[MOST * p : MOST * (p + 1), :] for w in whole], axis=0)
-        start = pl.multiple_of((minor[p] * 2 + c) * slab, 16)
-        cand[p, major[p], pl.ds(start, slab), :] = packed.astype(jnp.bfloat16)
+        rows8 = [ours[p * (nz // 2) + t].astype(jnp.float32) for t in range(nz // 2)]
+        packed = [jnp.concatenate([r[:8], r[8:]], axis=1) for r in rows8]
+        start = pl.multiple_of(minor[p] * slab, 16)
+        cand[p, c, major[p], pl.ds(start, slab), :] = jnp.concatenate(packed, axis=0).astype(
+            jnp.bfloat16
+        )
 
     def slab_at(p, a, b, core):
-        start = pl.multiple_of((b * 2 + core) * slab, 16)
-        return cand.at[p, a, pl.ds(start, slab), :]
+        start = pl.multiple_of(b * slab, 16)
+        return cand.at[p, core, a, pl.ds(start, slab), :]
 
     def spot(p, a, b):
         return (b, a) if p == 0 else (a, b)
 
     def copy(p, a, b, core, ssem, rsem, target):
         ref = slab_at(p, a, b, core)
-        return pltpu.make_async_remote_copy(
-            src_ref=ref, dst_ref=ref, send_sem=ssem, recv_sem=rsem,
-            device_id=target, device_id_type=MESH)
+        return remote(ref, ref, ssem, rsem, target)
 
     def major_copy(p, k):
         a, b = major[p], minor[p]
@@ -154,44 +237,45 @@
                 minor_copy(p, a, j).start()
             core_copy(p, a, minor[p]).start()
 
-    def turn_at(p, k):
-        return (major[p] + k + (k // 2) * (1 - 2 * (k % 2))) % 4
-
     def pass_on(p, k):
-        a = turn_at(p, k)
+        a = (major[p] + k) % 4
         for j in (1, 3, 2):
             b = (minor[p] + j) % 4
             slab_arrival(p, a, b).wait_recv()
             core_copy(p, a, b).start()
 
-    def absorb(p, k):
-        a = turn_at(p, k)
-        for b in range(4):
-            core_arrival(p, a, b).wait_recv()
-        block = cand[p, a]
-        wide = block.astype(jnp.float32)
-        norm = jnp.sum(wide * wide, axis=1, keepdims=True) * 0.25
+    def absorb(p, ks_):
+        at = [(major[p] + k) % 4 for k in ks_]
+        for a in at:
+            for b in range(4):
+                core_arrival(p, a, b).wait_recv()
+        blocks = [jnp.concatenate([cand[p, h, a] for a in at], axis=0) for h in range(2)]
+        wide = [block.astype(jnp.float32) for block in blocks]
+        norm = jnp.sum(wide[0] * wide[0] + wide[1] * wide[1], axis=1, keepdims=True) * 0.25
         for j in range(rows // TILE):
             lanes = slice(TILE * j, TILE * (j + 1))
             mine = emb[TILE // 16 * j : TILE // 16 * (j + 1)].reshape(TILE, -1)
-            product = lax.dot_general(block, mine, NT, preferred_element_type=jnp.float32)
+            product = sum(
+                lax.dot_general(
+                    blocks[h], mine[:, half * h : half * (h + 1)], NT,
+                    preferred_element_type=jnp.float32)
+                for h in range(2)
+            )
             reach = (product + norm).reshape(-1, 8, TILE)
             least[p, :, lanes] = jnp.minimum(least[p, :, lanes], jnp.min(reach, axis=0))
 
-    for p in range(2):
-        pass_on(p, 0)
-
-    def step(k, _):
+    for k in (0, 1):
         for p in range(2):
-            absorb(p, k)
-
-            @pl.when(k < 3)
-            def _():
-                pass_on(p, k + 1)
-
-        return 0
-
-    lax.fori_loop(0, 4, step, 0)
+            pass_on(p, k)
+    absorb(0, (0, 1))
+    pass_on(0, 3)
+    pass_on(1, 3)
+    absorb(1, (0, 1))
+    pass_on(0, 2)
+    pass_on(1, 2)
+    absorb(0, (3, 2))
+    absorb(1, (3, 2))
+    load_near.wait()
 
     norms = out_ref[...]
     near = near_ref[...]
@@ -203,7 +287,6 @@
     lane = lax.broadcasted_iota(jnp.int32, (1, 128), 1)
     share = jnp.where(lane == 0, sums[0], jnp.where(lane == 1, sums[1], 0.0))
 
-    at_z = z * 2 + c
     sum_z[at_z] = share
     for i, (tz, tc) in enumerate(column):
         pltpu.make_async_remote_copy(
@@ -215,13 +298,16 @@
         pltpu.make_async_remote_copy(
             src_ref=sum_z.at[t], dst_ref=sum_z.at[t], send_sem=azs.at[i],
             recv_sem=azr.at[t], device_id=device(x, y, tc, tz), device_id_type=MESH).wait_recv()
-    at_xy = x * NY + y
     sum_xy[at_xy] = jnp.sum(sum_z[...], axis=0)
     for i, (tx, ty) in enumerate(plane):
         pltpu.make_async_remote_copy(
             src_ref=sum_xy.at[at_xy], dst_ref=sum_xy.at[at_xy], send_sem=axs.at[i],
             recv_sem=axr.at[at_xy], device_id=device(tx, ty, c, z), device_id_type=MESH).start()
 
+    for i in range(len(column)):
+        slots_copy(i).wait_send()
+    for i in range(len(plane)):
+        part_copy(i).wait_send()
     for k in range(1, nz):
         z_copy(k).wait_send()
     for p in range(2):
@@ -262,8 +348,8 @@
             jax.ShapeDtypeStruct((2,), jnp.float32),
         ),
         in_specs=[
-            pl.BlockSpec(memory_space=pltpu.VMEM),
-            pl.BlockSpec(memory_space=pltpu.VMEM),
+            pl.BlockSpec(memory_space=pl.ANY),
+            pl.BlockSpec(memory_space=pl.ANY),
             pl.BlockSpec(memory_space=pl.ANY),
         ],
         out_specs=(
@@ -271,13 +357,23 @@
             pl.BlockSpec(memory_space=pltpu.SMEM),
         ),
         scratch_shapes=[
+            pltpu.VMEM(chosen.shape, jnp.int32),
+            pltpu.VMEM((1, rows), jnp.float32),
             pltpu.VMEM((rows // 16, 16, width), jnp.bfloat16),
-            pltpu.VMEM((nz, 16, width), jnp.bfloat16),
-            pltpu.VMEM((2, 4, 8 * nz * MOST, width), jnp.bfloat16),
+            pltpu.VMEM((2, 16, 3 * width // 8), jnp.bfloat16),
+            pltpu.VMEM((2 * nz, 16, 3 * width // 8), jnp.bfloat16),
+            pltpu.VMEM((NX * NY, 16, width // 4), jnp.bfloat16),
+            pltpu.VMEM((NX * NY, 16, width // 4), jnp.bfloat16),
+            pltpu.VMEM((nz, 16, width // 4), jnp.bfloat16),
+            pltpu.VMEM((2, 2, 4, 16 * nz, width // 2), jnp.bfloat16),
             pltpu.VMEM((2, 8, rows), jnp.float32),
             pltpu.VMEM((2 * nz, 1, 128), jnp.float32),
             pltpu.VMEM((NX * NY, 1, 128), jnp.float32),
-            dma,
+            dma((3,)),
+            dma((2 * nz - 1,)),
+            dma((2 * nz,)),
+            dma((NX * NY - 1,)),
+            dma((NX * NY,)),
             dma((nz - 1,)),
             dma((nz,)),
             dma((2, 3)),
@@ -291,10 +387,10 @@
             dma((NX * NY,)),
         ],
         compiler_params=pltpu.CompilerParams(
-            collective_id=0, has_side_effects=True, vmem_limit_bytes=40 * 2**20
+            collective_id=0, has_side_effects=True, vmem_limit_bytes=60 * 2**20
         ),
         cost_estimate=pl.CostEstimate(
-            flops=2 * rows * width * 3072, bytes_accessed=rows * width * 2, transcendentals=0
+            flops=4 * rows * width * chosen.shape[1], bytes_accessed=rows * width * 2, transcendentals=0
         ),
     )(chosen, nearest.reshape(1, rows), embeddings.reshape(rows // 16, 16, width))
     return near.reshape(rows), cost

time: 64.8 us -> 57.5 us (0.89)
  Pallas kernels: 59.3 us -> 54.3 us
  local copies, waits for them, and re-layouts: 4.68 us -> 2.43 us
    pallas_call x1, Pallas kernels: 59.3 us -> 54.3 us  [local(): pl.pallas_call(functools.partial(kernel, total_rows=total_rows), out_shap...]
    unnamed x8 -> x2, local copies, waits for them, and re-layouts: 4.68 us -> 2.43 us
where the time goes in v2:
time: 57.5 us; the launch traced here: 57.3 us
  Pallas kernels  54.3 us (94%)
  local copies, waits for them, and re-layouts  2.43 us (4%)
  between operations  0.64 us (1%)
    pallas_call x1, Pallas kernels, local(): pl.pallas_call(functools.partial(kernel, total_rows=total_rows), out_shap...  54.3 us
    unnamed x2, local copies, waits for them, and re-layouts  2.43 us

profile of v2, /device:TPU:1, one launch (start us, length us, event | category | flops | bytes accessed | tf_op | source)
XLA Modules:
  0.0 57.3 jit_solution(8006232129749267373)
XLA Ops:
  0.6 54.3 %shard_map.50 = (f32[1,2048]{1,0:T(1,128)}, f32[2]{0:T(128)}) custom-call(s32[2,512]{1,0:T(2,128)} %chosen_hbm.1, f32[1,2048]{1,0:T(1,128)} %bitcast.5, bf16[128,16,1024]{2,1,0:T(8,128)(2,1)} %bitcast.4), custom_call_target="tpu_custom_call" | custom-call | flops 4294967296 | bytes 4194304 | tf_op jit(solution)/shard_map/pallas_call | solution.py:344
  54.9 1.3 %copy.7 = f32[2048]{0:T(1024)} copy(f32[2048]{0:T(1024)} %bitcast.3) | data formatting | bytes 16384
  56.2 1.1 %copy.8 = f32[2]{0:T(128)} copy(f32[2]{0:T(128)} %get-tuple-element.9) | data formatting | bytes 16

commit v3 on v2

--- a/solution.py
+++ b/solution.py
@@ -13,6 +13,14 @@
 MOST = 6
 NONE = 2**30
 TILE = 256
+
+
+def far_first(sizes):
+    steps = [(a, b) for a in range(sizes[0]) for b in range(sizes[1]) if a or b]
+    return sorted(steps, key=lambda s: -sum(min(a, n - a) for a, n in zip(s, sizes)))
+
+
+PLANE = far_first((NX, NY))
 
 
 def place():
@@ -96,8 +104,8 @@
     load.start()
     load_near.start()
 
-    column = [((z + dz) % nz, (c + dc) % 2) for dz in range(nz) for dc in range(2) if dz or dc]
-    plane = [((x + dx) % NX, (y + dy) % NY) for dx in range(NX) for dy in range(NY) if dx or dy]
+    column = [((z + dz) % nz, (c + dc) % 2) for dz, dc in far_first((nz, 2))]
+    plane = [((x + dx) % NX, (y + dy) % NY) for dx, dy in PLANE]
     barrier = pltpu.get_barrier_semaphore()
     for tz, tc in column:
         pl.semaphore_signal(barrier, inc=1, device_id=device(x, y, tc, tz), device_id_type=MESH)
@@ -130,8 +138,7 @@
         t = tz * 2 + tc
         return remote(sent.at[tc], col.at[t], zs.at[i], zr.at[t], device(x, y, tc, tz))
 
-    far_first = sorted(range(len(column)), key=lambda i: abs((i + 1) // 2 - nz // 2))
-    for i in far_first:
+    for i in range(len(column)):
         slots_copy(i).start()
 
     for j in range(rows // 128):
@@ -244,12 +251,12 @@
             slab_arrival(p, a, b).wait_recv()
             core_copy(p, a, b).start()
 
-    def absorb(p, ks_):
-        at = [(major[p] + k) % 4 for k in ks_]
-        for a in at:
+    def absorb(k):
+        at = [(major[p] + k) % 4 for p in range(2)]
+        for p in range(2):
             for b in range(4):
-                core_arrival(p, a, b).wait_recv()
-        blocks = [jnp.concatenate([cand[p, h, a] for a in at], axis=0) for h in range(2)]
+                core_arrival(p, at[p], b).wait_recv()
+        blocks = [jnp.concatenate([cand[p, h, at[p]] for p in range(2)], axis=0) for h in range(2)]
         wide = [block.astype(jnp.float32) for block in blocks]
         norm = jnp.sum(wide[0] * wide[0] + wide[1] * wide[1], axis=1, keepdims=True) * 0.25
         for j in range(rows // TILE):
@@ -261,20 +268,21 @@
                     preferred_element_type=jnp.float32)
                 for h in range(2)
             )
-            reach = (product + norm).reshape(-1, 8, TILE)
-            least[p, :, lanes] = jnp.minimum(least[p, :, lanes], jnp.min(reach, axis=0))
-
-    for k in (0, 1):
+            reach = jnp.min((product + norm).reshape(2, -1, 8, TILE), axis=1)
+            least[:, :, lanes] = jnp.minimum(least[:, :, lanes], reach)
+
+    def pass_both(k):
         for p in range(2):
             pass_on(p, k)
-    absorb(0, (0, 1))
-    pass_on(0, 3)
-    pass_on(1, 3)
-    absorb(1, (0, 1))
-    pass_on(0, 2)
-    pass_on(1, 2)
-    absorb(0, (3, 2))
-    absorb(1, (3, 2))
+
+    pass_both(0)
+    absorb(0)
+    pass_both(1)
+    pass_both(3)
+    absorb(1)
+    pass_both(2)
+    absorb(3)
+    absorb(2)
     load_near.wait()
 
     norms = out_ref[...]

time: 57.5 us -> 55 us (0.957)
  Pallas kernels: 54.3 us -> 51.7 us
    pallas_call x1, Pallas kernels: 54.3 us -> 51.7 us  [local(): pl.pallas_call(functools.partial(kernel, total_rows=total_rows), out_shap...]
where the time goes in v3:
time: 55 us; the launch traced here: 54.8 us
  Pallas kernels  51.7 us (94%)
  local copies, waits for them, and re-layouts  2.43 us (4%)
  between operations  0.64 us (1%)
    pallas_call x1, Pallas kernels, local(): pl.pallas_call(functools.partial(kernel, total_rows=total_rows), out_shap...  51.7 us
    unnamed x2, local copies, waits for them, and re-layouts  2.43 us

profile of v3, /device:TPU:1, one launch (start us, length us, event | category | flops | bytes accessed | tf_op | source)
XLA Modules:
  0.0 54.8 jit_solution(214883523165874650)
XLA Ops:
  0.6 51.7 %shard_map.50 = (f32[1,2048]{1,0:T(1,128)}, f32[2]{0:T(128)}) custom-call(s32[2,512]{1,0:T(2,128)} %chosen_hbm.1, f32[1,2048]{1,0:T(1,128)} %bitcast.5, bf16[128,16,1024]{2,1,0:T(8,128)(2,1)} %bitcast.4), custom_call_target="tpu_custom_call" | custom-call | flops 4294967296 | bytes 4194304 | tf_op jit(solution)/shard_map/pallas_call | solution.py:352
  52.4 1.3 %copy.7 = f32[2048]{0:T(1024)} copy(f32[2048]{0:T(1024)} %bitcast.3) | data formatting | bytes 16384
  53.7 1.1 %copy.8 = f32[2]{0:T(128)} copy(f32[2]{0:T(128)} %get-tuple-element.9) | data formatting | bytes 16

commit v4 on v3

--- a/solution.py
+++ b/solution.py
@@ -83,8 +83,8 @@
 
 
 def kernel(
-    chosen_hbm, near_hbm, emb_hbm, out_ref, cost_ref,
-    chosen_ref, near_ref, emb, sent, col, parts, shares, ours, cand, least, sum_z, sum_xy,
+    chosen_hbm, near_hbm, emb_hbm, result,
+    out_ref, chosen_ref, near_ref, emb, sent, col, parts, shares, ours, cand, least, sum_z, sum_xy,
     in_sem, zs, zr, ps, pr, os, orr, bs, cs, ks, slab_r, sib_r, azs, azr, axs, axr, total_rows,
 ):
     x, y, c, z = place()
@@ -220,14 +220,16 @@
         tx, ty = spot(p, major[p], (b + k) % 4)
         return copy(p, a, b, c, cs.at[p, a, k - 1], slab_r.at[p, a, b], device(tx, ty, c, z))
 
-    def core_copy(p, a, b):
-        return copy(p, a, b, c, ks.at[p, a, b], sib_r.at[p, a, b], device(x, y, 1 - c, z))
+    def core_copy(p, a):
+        ref = cand.at[p, c, a]
+        return remote(ref, ref, ks.at[p, a], sib_r.at[p, a], device(x, y, 1 - c, z))
 
     def slab_arrival(p, a, b):
-        return copy(p, a, b, c, ks.at[p, a, b], slab_r.at[p, a, b], device(x, y, 1 - c, z))
-
-    def core_arrival(p, a, b):
-        return copy(p, a, b, 1 - c, ks.at[p, a, b], sib_r.at[p, a, b], device(x, y, 1 - c, z))
+        return copy(p, a, b, c, ks.at[p, a], slab_r.at[p, a, b], device(x, y, 1 - c, z))
+
+    def core_arrival(p, a):
+        ref = cand.at[p, 1 - c, a]
+        return remote(ref, ref, ks.at[p, a], sib_r.at[p, a], device(x, y, 1 - c, z))
 
     for k in (2, 1, 3):
         for p in range(2):
@@ -235,27 +237,24 @@
     for p in range(2):
         for k in (2, 1, 3):
             minor_copy(p, major[p], k).start()
-        core_copy(p, major[p], minor[p]).start()
     for k in (1, 3, 2):
         for p in range(2):
             a = (major[p] + k) % 4
             slab_arrival(p, a, minor[p]).wait_recv()
             for j in (2, 1, 3):
                 minor_copy(p, a, j).start()
-            core_copy(p, a, minor[p]).start()
 
     def pass_on(p, k):
         a = (major[p] + k) % 4
         for j in (1, 3, 2):
             b = (minor[p] + j) % 4
             slab_arrival(p, a, b).wait_recv()
-            core_copy(p, a, b).start()
+        core_copy(p, a).start()
 
     def absorb(k):
         at = [(major[p] + k) % 4 for p in range(2)]
         for p in range(2):
-            for b in range(4):
-                core_arrival(p, at[p], b).wait_recv()
+            core_arrival(p, at[p]).wait_recv()
         blocks = [jnp.concatenate([cand[p, h, at[p]] for p in range(2)], axis=0) for h in range(2)]
         wide = [block.astype(jnp.float32) for block in blocks]
         norm = jnp.sum(wide[0] * wide[0] + wide[1] * wide[1], axis=1, keepdims=True) * 0.25
@@ -301,6 +300,8 @@
             src_ref=sum_z.at[at_z], dst_ref=sum_z.at[at_z], send_sem=azs.at[i],
             recv_sem=azr.at[at_z], device_id=device(x, y, tc, tz), device_id_type=MESH).start()
     out_ref[...] = near
+    store = pltpu.make_async_copy(out_ref, result.at[:, pl.ds(0, rows)], in_sem.at[0])
+    store.start()
     for i, (tz, tc) in enumerate(column):
         t = tz * 2 + tc
         pltpu.make_async_remote_copy(
@@ -324,8 +325,7 @@
         for a in range(4):
             for k in (1, 2, 3):
                 minor_copy(p, a, k).wait_send()
-            for b in range(4):
-                core_copy(p, a, b).wait_send()
+            core_copy(p, a).wait_send()
     for i, (tz, tc) in enumerate(column):
         pltpu.make_async_remote_copy(
             src_ref=sum_z.at[at_z], dst_ref=sum_z.at[at_z], send_sem=azs.at[i],
@@ -338,9 +338,18 @@
             recv_sem=axr.at[t], device_id=device(tx, ty, c, z), device_id_type=MESH)
         both.wait_recv()
         both.wait_send()
-    final = jnp.sum(sum_xy[...], axis=0) / total_rows
-    cost_ref[0] = final[0, 0]
-    cost_ref[1] = final[0, 1]
+    sum_xy[0] = jnp.sum(sum_xy[...], axis=0) / total_rows
+    last = pltpu.make_async_copy(sum_xy.at[0], result.at[:, pl.ds(rows, 128)], in_sem.at[1])
+    last.start()
+    store.wait()
+    last.wait()
+
+
+def finish(result, near_out, cost_out):
+    rows = near_out.shape[1]
+    near_out[...] = result[:, :rows]
+    cost_out[0] = result[0, rows]
+    cost_out[1] = result[0, rows + 1]
 
 
 def local(embeddings, nearest, chosen):
@@ -349,22 +358,17 @@
     total_rows = rows * nz * lax.axis_size("group")
     dma = pltpu.SemaphoreType.DMA
 
-    near, cost = pl.pallas_call(
+    result = pl.pallas_call(
         functools.partial(kernel, total_rows=total_rows),
-        out_shape=(
-            jax.ShapeDtypeStruct((1, rows), jnp.float32),
-            jax.ShapeDtypeStruct((2,), jnp.float32),
-        ),
+        out_shape=jax.ShapeDtypeStruct((1, rows + 128), jnp.float32),
         in_specs=[
             pl.BlockSpec(memory_space=pl.ANY),
             pl.BlockSpec(memory_space=pl.ANY),
             pl.BlockSpec(memory_space=pl.ANY),
         ],
-        out_specs=(
-            pl.BlockSpec(memory_space=pltpu.VMEM),
-            pl.BlockSpec(memory_space=pltpu.SMEM),
-        ),
+        out_specs=pl.BlockSpec(memory_space=pl.ANY),
         scratch_shapes=[
+            pltpu.VMEM((1, rows), jnp.float32),
             pltpu.VMEM(chosen.shape, jnp.int32),
             pltpu.VMEM((1, rows), jnp.float32),
             pltpu.VMEM((rows // 16, 16, width), jnp.bfloat16),
@@ -386,9 +390,9 @@
             dma((nz,)),
             dma((2, 3)),
             dma((2, 4, 3)),
+            dma((2, 4)),
             dma((2, 4, 4)),
-            dma((2, 4, 4)),
-            dma((2, 4, 4)),
+            dma((2, 4)),
             dma((2 * nz - 1,)),
             dma((2 * nz,)),
             dma((NX * NY - 1,)),
@@ -401,6 +405,21 @@
             flops=4 * rows * width * chosen.shape[1], bytes_accessed=rows * width * 2, transcendentals=0
         ),
     )(chosen, nearest.reshape(1, rows), embeddings.reshape(rows // 16, 16, width))
+    near, cost = pl.pallas_call(
+        finish,
+        out_shape=(
+            jax.ShapeDtypeStruct((1, rows), jnp.float32),
+            jax.ShapeDtypeStruct((2,), jnp.float32),
+        ),
+        in_specs=[
+            pl.BlockSpec(memory_space=pltpu.VMEM),
+        ],
+        out_specs=(
+            pl.BlockSpec(memory_space=pltpu.VMEM),
+            pl.BlockSpec(memory_space=pltpu.SMEM),
+        ),
+        compiler_params=pltpu.CompilerParams(vmem_limit_bytes=60 * 2**20),
+    )(result)
     return near.reshape(rows), cost
 
 

time: 55 us -> 53.5 us (0.973)
  local copies, waits for them, and re-layouts: 2.43 us -> 0 us
  Pallas kernels: 51.7 us -> 52.7 us
    unnamed x2 -> x0, local copies, waits for them, and re-layouts: 2.43 us -> none
    pallas_call x0 -> x1, Pallas kernels: none -> 1.32 us  [local(): pl.pallas_call(finish, out_shape=(jax.ShapeDtypeStruct((1, rows), jnp.flo...]
where the time goes in v4:
time: 53.5 us; the launch traced here: 53.4 us
  Pallas kernels  52.7 us (99%)
  between operations  0.64 us (1%)
    pallas_call x1, Pallas kernels, local(): pl.pallas_call(functools.partial(kernel, total_rows=total_rows), out_shap...  51.4 us
    pallas_call x1, Pallas kernels, local(): pl.pallas_call(finish, out_shape=(jax.ShapeDtypeStruct((1, rows), jnp.flo...  1.32 us

profile of v4, /device:TPU:1, one launch (start us, length us, event | category | flops | bytes accessed | tf_op | source)
XLA Modules:
  0.0 53.4 jit_solution(1738218550404668248)
XLA Ops:
  0.6 51.4 %shard_map.50.result = f32[1,2176]{1,0:T(1,128)} custom-call(s32[2,512]{1,0:T(2,128)} %chosen_hbm.1, f32[1,2048]{1,0:T(1,128)} %bitcast.4, bf16[128,16,1024]{2,1,0:T(8,128)(2,1)} %bitcast.3), custom_call_target="tpu_custom_call" | custom-call | flops 4294967296 | bytes 4194304 | tf_op jit(solution)/shard_map/pallas_call | solution.py:361
  52.0 1.3 %shard_map.51 = (f32[1,2048]{1,0:T(1,128)}, f32[2]{0:T(128)}) custom-call(f32[1,2176]{1,0:T(1,128)} %shard_map.50.result), custom_call_target="tpu_custom_call" | custom-call | tf_op jit(solution)/shard_map/pallas_call | solution.py:408

commit v5 on v4

--- a/solution.py
+++ b/solution.py
@@ -1,4 +1,5 @@
 import functools
+import itertools
 
 import jax
 import jax.numpy as jnp
@@ -16,7 +17,7 @@
 
 
 def far_first(sizes):
-    steps = [(a, b) for a in range(sizes[0]) for b in range(sizes[1]) if a or b]
+    steps = [s for s in itertools.product(*map(range, sizes)) if any(s)]
     return sorted(steps, key=lambda s: -sum(min(a, n - a) for a, n in zip(s, sizes)))
 
 
@@ -84,8 +85,8 @@
 
 def kernel(
     chosen_hbm, near_hbm, emb_hbm, result,
-    out_ref, chosen_ref, near_ref, emb, sent, col, parts, shares, ours, cand, least, sum_z, sum_xy,
-    in_sem, zs, zr, ps, pr, os, orr, bs, cs, ks, slab_r, sib_r, azs, azr, axs, axr, total_rows,
+    out_ref, chosen_ref, near_ref, emb, sent, col, parts, shares, ours, cand, least, sums_at, total,
+    in_sem, zs, zr, ps, pr, os, orr, bs, cs, ks, slab_r, sib_r, sum_sem, total_rows,
 ):
     x, y, c, z = place()
     nz = lax.axis_size("dev")
@@ -294,24 +295,16 @@
     lane = lax.broadcasted_iota(jnp.int32, (1, 128), 1)
     share = jnp.where(lane == 0, sums[0], jnp.where(lane == 1, sums[1], 0.0))
 
-    sum_z[at_z] = share
-    for i, (tz, tc) in enumerate(column):
-        pltpu.make_async_remote_copy(
-            src_ref=sum_z.at[at_z], dst_ref=sum_z.at[at_z], send_sem=azs.at[i],
-            recv_sem=azr.at[at_z], device_id=device(x, y, tc, tz), device_id_type=MESH).start()
+    sums_at[position] = share
+    everyone = far_first((NX, NY, nz, 2))
+    xs, ys = [(x + i) % NX for i in range(NX)], [(y + i) % NY for i in range(NY)]
+    zs_, cores = [(z + i) % nz for i in range(nz)], [c, 1 - c]
+    for dx, dy, dz, dc in everyone:
+        target = device(xs[dx], ys[dy], cores[dc], zs_[dz])
+        remote(sums_at.at[position], sums_at.at[position], sum_sem.at[0], sum_sem.at[1], target).start()
     out_ref[...] = near
     store = pltpu.make_async_copy(out_ref, result.at[:, pl.ds(0, rows)], in_sem.at[0])
     store.start()
-    for i, (tz, tc) in enumerate(column):
-        t = tz * 2 + tc
-        pltpu.make_async_remote_copy(
-            src_ref=sum_z.at[t], dst_ref=sum_z.at[t], send_sem=azs.at[i],
-            recv_sem=azr.at[t], device_id=device(x, y, tc, tz), device_id_type=MESH).wait_recv()
-    sum_xy[at_xy] = jnp.sum(sum_z[...], axis=0)
-    for i, (tx, ty) in enumerate(plane):
-        pltpu.make_async_remote_copy(
-            src_ref=sum_xy.at[at_xy], dst_ref=sum_xy.at[at_xy], send_sem=axs.at[i],
-            recv_sem=axr.at[at_xy], device_id=device(tx, ty, c, z), device_id_type=MESH).start()
 
     for i in range(len(column)):
         slots_copy(i).wait_send()
@@ -326,21 +319,13 @@
             for k in (1, 2, 3):
                 minor_copy(p, a, k).wait_send()
             core_copy(p, a).wait_send()
-    for i, (tz, tc) in enumerate(column):
-        pltpu.make_async_remote_copy(
-            src_ref=sum_z.at[at_z], dst_ref=sum_z.at[at_z], send_sem=azs.at[i],
-            recv_sem=azr.at[at_z], device_id=device(x, y, tc, tz), device_id_type=MESH).wait_send()
-
-    for i, (tx, ty) in enumerate(plane):
-        t = tx * NY + ty
-        both = pltpu.make_async_remote_copy(
-            src_ref=sum_xy.at[t], dst_ref=sum_xy.at[t], send_sem=axs.at[i],
-            recv_sem=axr.at[t], device_id=device(tx, ty, c, z), device_id_type=MESH)
-        both.wait_recv()
-        both.wait_send()
-    sum_xy[0] = jnp.sum(sum_xy[...], axis=0) / total_rows
-    last = pltpu.make_async_copy(sum_xy.at[0], result.at[:, pl.ds(rows, 128)], in_sem.at[1])
+    others = sums_at.at[pl.ds(0, len(everyone))]
+    both = remote(others, others, sum_sem.at[0], sum_sem.at[1], device(x, y, 1 - c, z))
+    both.wait_recv()
+    total[...] = jnp.sum(sums_at[...], axis=0) / total_rows
+    last = pltpu.make_async_copy(total, result.at[:, pl.ds(rows, 128)], in_sem.at[1])
     last.start()
+    both.wait_send()
     store.wait()
     last.wait()
 
@@ -379,8 +364,8 @@
             pltpu.VMEM((nz, 16, width // 4), jnp.bfloat16),
             pltpu.VMEM((2, 2, 4, 16 * nz, width // 2), jnp.bfloat16),
             pltpu.VMEM((2, 8, rows), jnp.float32),
-            pltpu.VMEM((2 * nz, 1, 128), jnp.float32),
-            pltpu.VMEM((NX * NY, 1, 128), jnp.float32),
+            pltpu.VMEM((2 * NX * NY * nz, 1, 128), jnp.float32),
+            pltpu.VMEM((1, 128), jnp.float32),
             dma((3,)),
             dma((2 * nz - 1,)),
             dma((2 * nz,)),
@@ -393,10 +378,7 @@
             dma((2, 4)),
             dma((2, 4, 4)),
             dma((2, 4)),
-            dma((2 * nz - 1,)),
-            dma((2 * nz,)),
-            dma((NX * NY - 1,)),
-            dma((NX * NY,)),
+            dma((2,)),
         ],
         compiler_params=pltpu.CompilerParams(
             collective_id=0, has_side_effects=True, vmem_limit_bytes=60 * 2**20

time: 53.5 us -> 52.8 us (0.987)
  Pallas kernels: 52.7 us -> 52 us
    pallas_call x1, Pallas kernels: 51.4 us -> 50.7 us  [local(): pl.pallas_call(functools.partial(kernel, total_rows=total_rows), out_shap...]
where the time goes in v5:
time: 52.8 us; the launch traced here: 52.6 us
  Pallas kernels  52 us (98%)
  between operations  0.64 us (1%)
    pallas_call x1, Pallas kernels, local(): pl.pallas_call(functools.partial(kernel, total_rows=total_rows), out_shap...  50.7 us
    pallas_call x1, Pallas kernels, local(): pl.pallas_call(finish, out_shape=(jax.ShapeDtypeStruct((1, rows), jnp.flo...  1.32 us

profile of v5, /device:TPU:1, one launch (start us, length us, event | category | flops | bytes accessed | tf_op | source)
XLA Modules:
  0.0 52.6 jit_solution(9207855128483057615)
XLA Ops:
  0.6 50.7 %shard_map.50.result = f32[1,2176]{1,0:T(1,128)} custom-call(s32[2,512]{1,0:T(2,128)} %chosen_hbm.1, f32[1,2048]{1,0:T(1,128)} %bitcast.4, bf16[128,16,1024]{2,1,0:T(8,128)(2,1)} %bitcast.3), custom_call_target="tpu_custom_call" | custom-call | flops 4294967296 | bytes 4194304 | tf_op jit(solution)/shard_map/pallas_call | solution.py:346
  51.3 1.3 %shard_map.51 = (f32[1,2048]{1,0:T(1,128)}, f32[2]{0:T(128)}) custom-call(f32[1,2176]{1,0:T(1,128)} %shard_map.50.result), custom_call_target="tpu_custom_call" | custom-call | tf_op jit(solution)/shard_map/pallas_call | solution.py:390

commit v6 on v5

--- a/solution.py
+++ b/solution.py
@@ -13,7 +13,7 @@
 NX, NY = 4, 4
 MOST = 6
 NONE = 2**30
-TILE = 256
+TILE = 512
 
 
 def far_first(sizes):
@@ -84,9 +84,9 @@
 
 
 def kernel(
-    chosen_hbm, near_hbm, emb_hbm, result,
-    out_ref, chosen_ref, near_ref, emb, sent, col, parts, shares, ours, cand, least, sums_at, total,
-    in_sem, zs, zr, ps, pr, os, orr, bs, cs, ks, slab_r, sib_r, sum_sem, total_rows,
+    chosen_hbm, near_hbm, emb_hbm, near_hbm_out, sums_hbm,
+    out_ref, chosen_ref, near_ref, emb, sent, col, parts, shares, ours, cand, least, share_ref,
+    in_sem, zs, zr, ps, pr, os, orr, bs, cs, ks, slab_r, sib_r, sum_sem,
 ):
     x, y, c, z = place()
     nz = lax.axis_size("dev")
@@ -295,15 +295,18 @@
     lane = lax.broadcasted_iota(jnp.int32, (1, 128), 1)
     share = jnp.where(lane == 0, sums[0], jnp.where(lane == 1, sums[1], 0.0))
 
-    sums_at[position] = share
+    share_ref[...] = share
+    mine_at = sums_hbm.at[pl.ds(position, 1)]
+    keep = pltpu.make_async_copy(share_ref, mine_at, in_sem.at[1])
     everyone = far_first((NX, NY, nz, 2))
     xs, ys = [(x + i) % NX for i in range(NX)], [(y + i) % NY for i in range(NY)]
     zs_, cores = [(z + i) % nz for i in range(nz)], [c, 1 - c]
     for dx, dy, dz, dc in everyone:
         target = device(xs[dx], ys[dy], cores[dc], zs_[dz])
-        remote(sums_at.at[position], sums_at.at[position], sum_sem.at[0], sum_sem.at[1], target).start()
+        remote(share_ref, mine_at, sum_sem.at[0], sum_sem.at[1], target).start()
+    keep.start()
     out_ref[...] = near
-    store = pltpu.make_async_copy(out_ref, result.at[:, pl.ds(0, rows)], in_sem.at[0])
+    store = pltpu.make_async_copy(out_ref, near_hbm_out, in_sem.at[0])
     store.start()
 
     for i in range(len(column)):
@@ -319,22 +322,19 @@
             for k in (1, 2, 3):
                 minor_copy(p, a, k).wait_send()
             core_copy(p, a).wait_send()
-    others = sums_at.at[pl.ds(0, len(everyone))]
+    others = sums_hbm.at[pl.ds(0, len(everyone))]
     both = remote(others, others, sum_sem.at[0], sum_sem.at[1], device(x, y, 1 - c, z))
+    keep.wait()
+    store.wait()
+    both.wait_send()
     both.wait_recv()
-    total[...] = jnp.sum(sums_at[...], axis=0) / total_rows
-    last = pltpu.make_async_copy(total, result.at[:, pl.ds(rows, 128)], in_sem.at[1])
-    last.start()
-    both.wait_send()
-    store.wait()
-    last.wait()
-
-
-def finish(result, near_out, cost_out):
-    rows = near_out.shape[1]
-    near_out[...] = result[:, :rows]
-    cost_out[0] = result[0, rows]
-    cost_out[1] = result[0, rows + 1]
+
+
+def finish(near_ref, sums_ref, near_out, cost_out, *, total_rows):
+    near_out[...] = near_ref[...]
+    total = jnp.sum(sums_ref[...], axis=0, keepdims=True) / total_rows
+    cost_out[0] = total[0, 0]
+    cost_out[1] = total[0, 1]
 
 
 def local(embeddings, nearest, chosen):
@@ -343,15 +343,21 @@
     total_rows = rows * nz * lax.axis_size("group")
     dma = pltpu.SemaphoreType.DMA
 
-    result = pl.pallas_call(
-        functools.partial(kernel, total_rows=total_rows),
-        out_shape=jax.ShapeDtypeStruct((1, rows + 128), jnp.float32),
+    near, sums = pl.pallas_call(
+        kernel,
+        out_shape=(
+            jax.ShapeDtypeStruct((1, rows), jnp.float32),
+            jax.ShapeDtypeStruct((total_rows // rows, 128), jnp.float32),
+        ),
         in_specs=[
             pl.BlockSpec(memory_space=pl.ANY),
             pl.BlockSpec(memory_space=pl.ANY),
             pl.BlockSpec(memory_space=pl.ANY),
         ],
-        out_specs=pl.BlockSpec(memory_space=pl.ANY),
+        out_specs=(
+            pl.BlockSpec(memory_space=pl.ANY),
+            pl.BlockSpec(memory_space=pl.ANY),
+        ),
         scratch_shapes=[
             pltpu.VMEM((1, rows), jnp.float32),
             pltpu.VMEM(chosen.shape, jnp.int32),
@@ -364,7 +370,6 @@
             pltpu.VMEM((nz, 16, width // 4), jnp.bfloat16),
             pltpu.VMEM((2, 2, 4, 16 * nz, width // 2), jnp.bfloat16),
             pltpu.VMEM((2, 8, rows), jnp.float32),
-            pltpu.VMEM((2 * NX * NY * nz, 1, 128), jnp.float32),
             pltpu.VMEM((1, 128), jnp.float32),
             dma((3,)),
             dma((2 * nz - 1,)),
@@ -388,12 +393,13 @@
         ),
     )(chosen, nearest.reshape(1, rows), embeddings.reshape(rows // 16, 16, width))
     near, cost = pl.pallas_call(
-        finish,
+        functools.partial(finish, total_rows=total_rows),
         out_shape=(
             jax.ShapeDtypeStruct((1, rows), jnp.float32),
             jax.ShapeDtypeStruct((2,), jnp.float32),
         ),
         in_specs=[
+            pl.BlockSpec(memory_space=pltpu.VMEM),
             pl.BlockSpec(memory_space=pltpu.VMEM),
         ],
         out_specs=(
@@ -401,7 +407,7 @@
             pl.BlockSpec(memory_space=pltpu.SMEM),
         ),
         compiler_params=pltpu.CompilerParams(vmem_limit_bytes=60 * 2**20),
-    )(result)
+    )(near, sums)
     return near.reshape(rows), cost
 
 

time: 52.8 us -> 52.3 us (level)
  no operation moved by 1% of the time
where the time goes in v6:
time: 52.3 us; the launch traced here: 52.1 us
  Pallas kernels  51.5 us (98%)
  between operations  0.64 us (1%)
    pallas_call x1, Pallas kernels, local(): pl.pallas_call(kernel, out_shape=(jax.ShapeDtypeStruct((1, rows), jnp.flo...  49.9 us
    pallas_call x1, Pallas kernels, local(): pl.pallas_call(functools.partial(finish, total_rows=total_rows), out_shap...  1.58 us

profile of v6, /device:TPU:1, one launch (start us, length us, event | category | flops | bytes accessed | tf_op | source)
XLA Modules:
  0.0 52.1 jit_solution(12285444688248380094)
XLA Ops:
  0.6 49.9 %shard_map.50 = (f32[1,2048]{1,0:T(1,128)}, f32[256,128]{1,0:T(8,128)}) custom-call(s32[2,512]{1,0:T(2,128)} %chosen_hbm.1, f32[1,2048]{1,0:T(1,128)} %bitcast.4, bf16[128,16,1024]{2,1,0:T(8,128)(2,1)} %bitcast.3), custom_call_target="tpu_custom_call" | custom-call | flops 4294967296 | bytes 4194304 | tf_op jit(solution)/shard_map/pallas_call | solution.py:346
  50.5 1.6 %shard_map.51 = (f32[1,2048]{1,0:T(1,128)}, f32[2]{0:T(128)}) custom-call(f32[1,2048]{1,0:T(1,128)} %get-tuple-element.6.near_ref, f32[256,128]{1,0:T(8,128)} %get-tuple-element.7.sums_ref), custom_call_target="tpu_custom_call" | custom-call | tf_op jit(solution)/shard_map/pallas_call | solution.py:395

commit v7 on v6

--- a/solution.py
+++ b/solution.py
@@ -86,7 +86,7 @@
 def kernel(
     chosen_hbm, near_hbm, emb_hbm, near_hbm_out, sums_hbm,
     out_ref, chosen_ref, near_ref, emb, sent, col, parts, shares, ours, cand, least, share_ref,
-    in_sem, zs, zr, ps, pr, os, orr, bs, cs, ks, slab_r, sib_r, sum_sem,
+    in_sem, zs, ps, os, bs, cs, ks, major_r, minor_r, sib_r, sum_sem,
 ):
     x, y, c, z = place()
     nz = lax.axis_size("dev")
@@ -130,17 +130,12 @@
             src_ref=src, dst_ref=dst, send_sem=ssem, recv_sem=rsem,
             device_id=target, device_id_type=MESH)
 
-    def slots_copy(i):
-        tz, tc = column[i]
-        return remote(sent.at[tc], col.at[at_z], zs.at[i], zr.at[at_z], device(x, y, tc, tz))
-
-    def slots_arrival(i):
-        tz, tc = column[i]
-        t = tz * 2 + tc
-        return remote(sent.at[tc], col.at[t], zs.at[i], zr.at[t], device(x, y, tc, tz))
-
-    for i in range(len(column)):
-        slots_copy(i).start()
+    def drain(ref, sems):
+        return remote(ref, ref, sems.at[0], sems.at[1], device(x, y, 1 - c, z))
+
+    for tz, tc in column:
+        remote(sent.at[tc], col.at[at_z], zs.at[0], zs.at[1], device(x, y, tc, tz)).start()
+    slots = drain(col.at[pl.ds(0, len(column))], zs)
 
     for j in range(rows // 128):
         part = emb[8 * j : 8 * (j + 1)].reshape(128, -1).astype(jnp.float32)
@@ -149,8 +144,7 @@
         out_ref[:, 128 * j : 128 * (j + 1)] = jnp.sum(part.T, axis=0, keepdims=True)
 
     main, tails = slot_sources(chosen_ref, x, y, z, rows, nz)
-    for i in range(len(column)):
-        slots_arrival(i).wait_recv()
+    slots.wait_recv()
 
     gathered = col[...].reshape(-1, cut)
     left = jnp.dot(main, gathered, preferred_element_type=jnp.float32)
@@ -165,33 +159,17 @@
         parts[t] = both.astype(jnp.bfloat16)
     shares[at_xy] = parts[at_xy]
 
-    def part_copy(i):
-        tx, ty = plane[i]
+    for tx, ty in plane:
         t = tx * NY + ty
-        return remote(parts.at[t], shares.at[at_xy], ps.at[i], pr.at[at_xy], device(tx, ty, c, z))
-
-    def part_arrival(i):
-        tx, ty = plane[i]
-        t = tx * NY + ty
-        return remote(parts.at[t], shares.at[t], ps.at[i], pr.at[t], device(tx, ty, c, z))
-
-    for i in range(len(plane)):
-        part_copy(i).start()
-    for i in range(len(plane)):
-        part_arrival(i).wait_recv()
+        remote(parts.at[t], shares.at[at_xy], ps.at[0], ps.at[1], device(tx, ty, c, z)).start()
+    part = drain(shares.at[pl.ds(0, len(plane))], ps)
+    part.wait_recv()
     ours[z] = jnp.sum(shares[...].astype(jnp.float32), axis=0).astype(jnp.bfloat16)
 
-    def z_copy(k):
-        return remote(ours.at[z], ours.at[z], os.at[k - 1], orr.at[z], device(x, y, c, (z + k) % nz))
-
-    def z_arrival(k):
-        t = (z + k) % nz
-        return remote(ours.at[t], ours.at[t], os.at[k - 1], orr.at[t], device(x, y, c, t))
-
     for k in (4, 3, 5, 2, 6, 1, 7):
-        z_copy(k).start()
-    for k in range(1, nz):
-        z_arrival(k).wait_recv()
+        remote(ours.at[z], ours.at[z], os.at[0], os.at[1], device(x, y, c, (z + k) % nz)).start()
+    along = drain(ours.at[pl.ds(0, nz - 1)], os)
+    along.wait_recv()
     for p in range(2):
         rows8 = [ours[p * (nz // 2) + t].astype(jnp.float32) for t in range(nz // 2)]
         packed = [jnp.concatenate([r[:8], r[8:]], axis=1) for r in rows8]
@@ -214,23 +192,27 @@
     def major_copy(p, k):
         a, b = major[p], minor[p]
         tx, ty = spot(p, (a + k) % 4, b)
-        return copy(p, a, b, c, bs.at[p, k - 1], slab_r.at[p, a, b], device(tx, ty, c, z))
+        return copy(p, a, b, c, bs.at[p], major_r.at[p, a], device(tx, ty, c, z))
 
     def minor_copy(p, a, k):
         b = minor[p]
         tx, ty = spot(p, major[p], (b + k) % 4)
-        return copy(p, a, b, c, cs.at[p, a, k - 1], slab_r.at[p, a, b], device(tx, ty, c, z))
+        return copy(p, a, b, c, cs.at[p], minor_r.at[p, a], device(tx, ty, c, z))
 
     def core_copy(p, a):
         ref = cand.at[p, c, a]
-        return remote(ref, ref, ks.at[p, a], sib_r.at[p, a], device(x, y, 1 - c, z))
-
-    def slab_arrival(p, a, b):
-        return copy(p, a, b, c, ks.at[p, a], slab_r.at[p, a, b], device(x, y, 1 - c, z))
+        return remote(ref, ref, ks.at[p], sib_r.at[p, a], device(x, y, 1 - c, z))
+
+    def major_arrival(p, a):
+        return copy(p, a, minor[p], c, bs.at[p], major_r.at[p, a], device(x, y, 1 - c, z))
+
+    def minor_arrivals(p, a):
+        ref = cand.at[p, c, a, pl.ds(0, 3 * slab)]
+        return remote(ref, ref, cs.at[p], minor_r.at[p, a], device(x, y, 1 - c, z))
 
     def core_arrival(p, a):
         ref = cand.at[p, 1 - c, a]
-        return remote(ref, ref, ks.at[p, a], sib_r.at[p, a], device(x, y, 1 - c, z))
+        return remote(ref, ref, ks.at[p], sib_r.at[p, a], device(x, y, 1 - c, z))
 
     for k in (2, 1, 3):
         for p in range(2):
@@ -241,15 +223,13 @@
     for k in (1, 3, 2):
         for p in range(2):
             a = (major[p] + k) % 4
-            slab_arrival(p, a, minor[p]).wait_recv()
+            major_arrival(p, a).wait_recv()
             for j in (2, 1, 3):
                 minor_copy(p, a, j).start()
 
     def pass_on(p, k):
         a = (major[p] + k) % 4
-        for j in (1, 3, 2):
-            b = (minor[p] + j) % 4
-            slab_arrival(p, a, b).wait_recv()
+        minor_arrivals(p, a).wait_recv()
         core_copy(p, a).start()
 
     def absorb(k):
@@ -309,19 +289,16 @@
     store = pltpu.make_async_copy(out_ref, near_hbm_out, in_sem.at[0])
     store.start()
 
-    for i in range(len(column)):
-        slots_copy(i).wait_send()
-    for i in range(len(plane)):
-        part_copy(i).wait_send()
-    for k in range(1, nz):
-        z_copy(k).wait_send()
+    slots.wait_send()
+    part.wait_send()
+    along.wait_send()
     for p in range(2):
-        for k in (1, 2, 3):
-            major_copy(p, k).wait_send()
-        for a in range(4):
-            for k in (1, 2, 3):
-                minor_copy(p, a, k).wait_send()
-            core_copy(p, a).wait_send()
+        three = cand.at[p, c, pl.ds(0, 3)]
+        first = cand.at[p, c, 0, pl.ds(0, 3 * slab)]
+        remote(first, first, bs.at[p], major_r.at[p, 0], device(x, y, 1 - c, z)).wait_send()
+        remote(three, three, cs.at[p], minor_r.at[p, 0], device(x, y, 1 - c, z)).wait_send()
+        four = cand.at[p, c]
+        remote(four, four, ks.at[p], sib_r.at[p, 0], device(x, y, 1 - c, z)).wait_send()
     others = sums_hbm.at[pl.ds(0, len(everyone))]
     both = remote(others, others, sum_sem.at[0], sum_sem.at[1], device(x, y, 1 - c, z))
     keep.wait()
@@ -372,16 +349,14 @@
             pltpu.VMEM((2, 8, rows), jnp.float32),
             pltpu.VMEM((1, 128), jnp.float32),
             dma((3,)),
-            dma((2 * nz - 1,)),
-            dma((2 * nz,)),
-            dma((NX * NY - 1,)),
-            dma((NX * NY,)),
-            dma((nz - 1,)),
-            dma((nz,)),
-            dma((2, 3)),
-            dma((2, 4, 3)),
+            dma((2,)),
+            dma((2,)),
+            dma((2,)),
+            dma((2,)),
+            dma((2,)),
+            dma((2,)),
             dma((2, 4)),
-            dma((2, 4, 4)),
+            dma((2, 4)),
             dma((2, 4)),
             dma((2,)),
         ],

time: 52.3 us -> 51.1 us (0.977)
  Pallas kernels: 51.5 us -> 50.3 us
    pallas_call x1, Pallas kernels: 49.9 us -> 48.7 us  [local(): pl.pallas_call(kernel, out_shape=(jax.ShapeDtypeStruct((1, rows), jnp.flo...]
where the time goes in v7:
time: 51.1 us; the launch traced here: 50.9 us
  Pallas kernels  50.3 us (98%)
  between operations  0.64 us (1%)
    pallas_call x1, Pallas kernels, local(): pl.pallas_call(kernel, out_shape=(jax.ShapeDtypeStruct((1, rows), jnp.flo...  48.7 us
    pallas_call x1, Pallas kernels, local(): pl.pallas_call(functools.partial(finish, total_rows=total_rows), out_shap...  1.58 us

profile of v7, /device:TPU:1, one launch (start us, length us, event | category | flops | bytes accessed | tf_op | source)
XLA Modules:
  0.0 50.9 jit_solution(5048570560751535388)
XLA Ops:
  0.6 48.7 %shard_map.50 = (f32[1,2048]{1,0:T(1,128)}, f32[256,128]{1,0:T(8,128)}) custom-call(s32[2,512]{1,0:T(2,128)} %chosen_hbm.1, f32[1,2048]{1,0:T(1,128)} %bitcast.4, bf16[128,16,1024]{2,1,0:T(8,128)(2,1)} %bitcast.3), custom_call_target="tpu_custom_call" | custom-call | flops 4294967296 | bytes 4194304 | tf_op jit(solution)/shard_map/pallas_call | solution.py:323
  49.3 1.6 %shard_map.51 = (f32[1,2048]{1,0:T(1,128)}, f32[2]{0:T(128)}) custom-call(f32[1,2048]{1,0:T(1,128)} %get-tuple-element.6.near_ref, f32[256,128]{1,0:T(8,128)} %get-tuple-element.7.sums_ref), custom_call_target="tpu_custom_call" | custom-call | tf_op jit(solution)/shard_map/pallas_call | solution.py:370

commit v8 on v7

--- a/solution.py
+++ b/solution.py
@@ -148,9 +148,9 @@
 
     gathered = col[...].reshape(-1, cut)
     left = jnp.dot(main, gathered, preferred_element_type=jnp.float32)
-    right = sum(
-        jnp.dot(tail, gathered[:, 128 * i : 128 * (i + 1)], preferred_element_type=jnp.float32)
-        for i, tail in enumerate(tails)
+    stacked = jnp.concatenate([gathered[:, 128 * i : 128 * (i + 1)] for i in range(3)], axis=0)
+    right = jnp.dot(
+        jnp.concatenate(tails, axis=1), stacked, preferred_element_type=jnp.float32
     )
     dense = jnp.concatenate([left, right], axis=1)
     for t in range(NX * NY):
@@ -178,33 +178,33 @@
             jnp.bfloat16
         )
 
-    def slab_at(p, a, b, core):
-        start = pl.multiple_of(b * slab, 16)
-        return cand.at[p, core, a, pl.ds(start, slab), :]
+    def slab_at(p, a, b, core, piece=None):
+        start, size = (b * slab, slab) if piece is None else (b * slab + 16 * piece, 16)
+        return cand.at[p, core, a, pl.ds(pl.multiple_of(start, 16), size), :]
 
     def spot(p, a, b):
         return (b, a) if p == 0 else (a, b)
 
-    def copy(p, a, b, core, ssem, rsem, target):
-        ref = slab_at(p, a, b, core)
+    def copy(p, a, b, core, ssem, rsem, target, piece=None):
+        ref = slab_at(p, a, b, core, piece)
         return remote(ref, ref, ssem, rsem, target)
 
-    def major_copy(p, k):
+    def major_copy(p, k, h):
         a, b = major[p], minor[p]
         tx, ty = spot(p, (a + k) % 4, b)
-        return copy(p, a, b, c, bs.at[p], major_r.at[p, a], device(tx, ty, c, z))
-
-    def minor_copy(p, a, k):
+        return copy(p, a, b, c, bs.at[p], major_r.at[p, a, h], device(tx, ty, c, z), h)
+
+    def minor_copy(p, a, k, h=None):
         b = minor[p]
         tx, ty = spot(p, major[p], (b + k) % 4)
-        return copy(p, a, b, c, cs.at[p], minor_r.at[p, a], device(tx, ty, c, z))
+        return copy(p, a, b, c, cs.at[p], minor_r.at[p, a], device(tx, ty, c, z), h)
 
     def core_copy(p, a):
         ref = cand.at[p, c, a]
         return remote(ref, ref, ks.at[p], sib_r.at[p, a], device(x, y, 1 - c, z))
 
-    def major_arrival(p, a):
-        return copy(p, a, minor[p], c, bs.at[p], major_r.at[p, a], device(x, y, 1 - c, z))
+    def major_arrival(p, a, h):
+        return copy(p, a, minor[p], c, bs.at[p], major_r.at[p, a, h], device(x, y, 1 - c, z), h)
 
     def minor_arrivals(p, a):
         ref = cand.at[p, c, a, pl.ds(0, 3 * slab)]
@@ -214,18 +214,19 @@
         ref = cand.at[p, 1 - c, a]
         return remote(ref, ref, ks.at[p], sib_r.at[p, a], device(x, y, 1 - c, z))
 
-    for k in (2, 1, 3):
-        for p in range(2):
-            major_copy(p, k).start()
+    for h in range(2):
+        for k in (2, 1, 3):
+            for p in range(2):
+                major_copy(p, k, h).start()
     for p in range(2):
         for k in (2, 1, 3):
             minor_copy(p, major[p], k).start()
-    for k in (1, 3, 2):
+    for k, h in ((1, 0), (3, 0), (1, 1), (3, 1), (2, 0), (2, 1)):
         for p in range(2):
             a = (major[p] + k) % 4
-            major_arrival(p, a).wait_recv()
+            major_arrival(p, a, h).wait_recv()
             for j in (2, 1, 3):
-                minor_copy(p, a, j).start()
+                minor_copy(p, a, j, h).start()
 
     def pass_on(p, k):
         a = (major[p] + k) % 4
@@ -256,8 +257,8 @@
             pass_on(p, k)
 
     pass_both(0)
+    pass_both(1)
     absorb(0)
-    pass_both(1)
     pass_both(3)
     absorb(1)
     pass_both(2)
@@ -295,7 +296,7 @@
     for p in range(2):
         three = cand.at[p, c, pl.ds(0, 3)]
         first = cand.at[p, c, 0, pl.ds(0, 3 * slab)]
-        remote(first, first, bs.at[p], major_r.at[p, 0], device(x, y, 1 - c, z)).wait_send()
+        remote(first, first, bs.at[p], major_r.at[p, 0, 0], device(x, y, 1 - c, z)).wait_send()
         remote(three, three, cs.at[p], minor_r.at[p, 0], device(x, y, 1 - c, z)).wait_send()
         four = cand.at[p, c]
         remote(four, four, ks.at[p], sib_r.at[p, 0], device(x, y, 1 - c, z)).wait_send()
@@ -355,7 +356,7 @@
             dma((2,)),
             dma((2,)),
             dma((2,)),
-            dma((2, 4)),
+            dma((2, 4, 2)),
             dma((2, 4)),
             dma((2, 4)),
             dma((2,)),

time: 51.1 us -> 50.8 us (level)
  no operation moved by 1% of the time
where the time goes in v8:
time: 50.8 us; the launch traced here: 50.6 us
  Pallas kernels  50 us (98%)
  between operations  0.64 us (1%)
    pallas_call x1, Pallas kernels, local(): pl.pallas_call(kernel, out_shape=(jax.ShapeDtypeStruct((1, rows), jnp.flo...  48.4 us
    pallas_call x1, Pallas kernels, local(): pl.pallas_call(functools.partial(finish, total_rows=total_rows), out_shap...  1.58 us

profile of v8, /device:TPU:1, one launch (start us, length us, event | category | flops | bytes accessed | tf_op | source)
XLA Modules:
  0.0 50.6 jit_solution(11792559157926906134)
XLA Ops:
  0.6 48.4 %shard_map.50 = (f32[1,2048]{1,0:T(1,128)}, f32[256,128]{1,0:T(8,128)}) custom-call(s32[2,512]{1,0:T(2,128)} %chosen_hbm.1, f32[1,2048]{1,0:T(1,128)} %bitcast.4, bf16[128,16,1024]{2,1,0:T(8,128)(2,1)} %bitcast.3), custom_call_target="tpu_custom_call" | custom-call | flops 4294967296 | bytes 4194304 | tf_op jit(solution)/shard_map/pallas_call | solution.py:324
  49.0 1.6 %shard_map.51 = (f32[1,2048]{1,0:T(1,128)}, f32[2]{0:T(128)}) custom-call(f32[1,2048]{1,0:T(1,128)} %get-tuple-element.6.near_ref, f32[256,128]{1,0:T(8,128)} %get-tuple-element.7.sums_ref), custom_call_target="tpu_custom_call" | custom-call | tf_op jit(solution)/shard_map/pallas_call | solution.py:371

commit v9 on v8

--- a/solution.py
+++ b/solution.py
@@ -308,11 +308,19 @@
     both.wait_recv()
 
 
-def finish(near_ref, sums_ref, near_out, cost_out, *, total_rows):
-    near_out[...] = near_ref[...]
+def finish(near_in, sums_in, near_out, cost_out, near_ref, sums_ref, sem, *, total_rows):
+    near_load = pltpu.make_async_copy(near_in, near_ref, sem.at[0])
+    sums_load = pltpu.make_async_copy(sums_in, sums_ref, sem.at[1])
+    near_store = pltpu.make_async_copy(near_ref, near_out, sem.at[2])
+    sums_load.start()
+    near_load.start()
+    near_load.wait()
+    near_store.start()
+    sums_load.wait()
     total = jnp.sum(sums_ref[...], axis=0, keepdims=True) / total_rows
     cost_out[0] = total[0, 0]
     cost_out[1] = total[0, 1]
+    near_store.wait()
 
 
 def local(embeddings, nearest, chosen):
@@ -375,13 +383,18 @@
             jax.ShapeDtypeStruct((2,), jnp.float32),
         ),
         in_specs=[
-            pl.BlockSpec(memory_space=pltpu.VMEM),
-            pl.BlockSpec(memory_space=pltpu.VMEM),
+            pl.BlockSpec(memory_space=pl.ANY),
+            pl.BlockSpec(memory_space=pl.ANY),
         ],
         out_specs=(
-            pl.BlockSpec(memory_space=pltpu.VMEM),
+            pl.BlockSpec(memory_space=pl.ANY),
             pl.BlockSpec(memory_space=pltpu.SMEM),
         ),
+        scratch_shapes=[
+            pltpu.VMEM((1, rows), jnp.float32),
+            pltpu.VMEM((total_rows // rows, 128), jnp.float32),
+            dma((3,)),
+        ],
         compiler_params=pltpu.CompilerParams(vmem_limit_bytes=60 * 2**20),
     )(near, sums)
     return near.reshape(rows), cost

time: 50.8 us -> 51.1 us (level)
  no operation moved by 1% of the time
where the time goes in v9:
time: 51.1 us; the launch traced here: 50.9 us
  Pallas kernels  50.3 us (98%)
  between operations  0.64 us (1%)
    pallas_call x1, Pallas kernels, local(): pl.pallas_call(kernel, out_shape=(jax.ShapeDtypeStruct((1, rows), jnp.flo...  48.4 us
    pallas_call x1, Pallas kernels, local(): pl.pallas_call(functools.partial(finish, total_rows=total_rows), out_shap...  1.9 us

profile of v9, /device:TPU:1, one launch (start us, length us, event | category | flops | bytes accessed | tf_op | source)
XLA Modules:
  0.0 50.9 jit_solution(16339203270298789277)
XLA Ops:
  0.6 48.4 %shard_map.50 = (f32[1,2048]{1,0:T(1,128)}, f32[256,128]{1,0:T(8,128)}) custom-call(s32[2,512]{1,0:T(2,128)} %chosen_hbm.1, f32[1,2048]{1,0:T(1,128)} %bitcast.4, bf16[128,16,1024]{2,1,0:T(8,128)(2,1)} %bitcast.3), custom_call_target="tpu_custom_call" | custom-call | flops 4294967296 | bytes 4194304 | tf_op jit(solution)/shard_map/pallas_call | solution.py:332
  49.0 1.9 %shard_map.51 = (f32[1,2048]{1,0:T(1,128)}, f32[2]{0:T(128)}) custom-call(f32[1,2048]{1,0:T(1,128)} %get-tuple-element.6.near_in, f32[256,128]{1,0:T(8,128)} %get-tuple-element.7.sums_in), custom_call_target="tpu_custom_call" | custom-call | tf_op jit(solution)/shard_map/pallas_call | solution.py:379
